TPU v7x, 512 devices: a whole 4x8x8 slice. The times are simulated.
512 devices in a mesh: dp: 8 (over y), fsdp: 8 (over x, z_lo), tensor: 8 (over z_hi, core).
Axes of the slice: x: 4, y: 8, z: 8 (z_hi: 4, z_lo: 2; z = z_hi * 2 + z_lo), core: 2. Of those that a mesh axis runs over, the one named last changes fastest.
Arguments:
- teacher_in: bfloat16 [16384, 4096], P(('dp', 'fsdp'), 'tensor'), may hold values from -6 to 6
- codes: int32 [4096, 1024], P('tensor'), may hold values from 0 to 65535
- scales: bfloat16 [32, 4096], P('tensor'), may hold values from 0.0019989014 to 0.0079956055
- teacher_resid: bfloat16 [16384, 8, 512], P(('dp', 'fsdp'), None, 'tensor'), may hold values from -48 to 48
- teacher_gain: bfloat16 [8, 512], P(None, 'tensor'), may hold values from 0.5 to 1.5
- projector: bfloat16 [8, 512, 1792], P('fsdp', 'tensor'), may hold values from -0.09375 to 0.09375
- routes: int32 [2048, 1], replicated, may hold values from 0 to 7; in each aligned block of 4 rows (0 to 3, 4 to 7, ...) no two rows name the same one
- student_in: bfloat16 [131072, 1792], P(('dp', 'fsdp', 'tensor')), may hold values from -6 to 6
- queries: bfloat16 [131072, 1792], P(('dp', 'fsdp', 'tensor')), may hold values from -6 to 6
- keys: bfloat16 [131072, 256], P(('dp', 'fsdp', 'tensor')), may hold values from -6 to 6
- segments: int32 [131072], P(('dp', 'fsdp', 'tensor')), may hold values from 0 to 8191, never falling along the last dimension, each value on 1 to 128 neighbouring positions
- value_weight: bfloat16 [1792, 256], P(('fsdp', 'tensor')), may hold values from -0.125 to 0.125
Outputs:
- loss: float32 [], replicated
- grad_value: float32 [1792, 256], P(('fsdp', 'tensor'))
Inputs may be any that keep to these rules, and one draw needn't show every extreme that they name: `routes`: each row names the student data group of one teacher block of 8 rows; the 4 blocks of one device go to different groups. `segments`: document ids never fall along the rows; each document has at most 128 tokens.
All inputs are finite; a program needn't handle non-finite values.
Results may differ from a plain program's by a relative error of at most 0.0055.
Values may be sent and summed in bfloat16 or wider, within the bound.
A program may use at most 64 MiB of HBM per device.

v0:
```python
import jax
import jax.numpy as jnp
from jax import lax
from jax.sharding import PartitionSpec as P

HT = 4096
GROUP = 128
HEAD = 128


EPS = 1e-06


def unpack_levels(codes):
    pieces = [
        jnp.bitwise_and(jnp.right_shift(codes, 4 * shift_step), 15) for shift_step in range(4)
    ]
    stacked = jnp.stack(pieces, axis=-1)
    return stacked.reshape(codes.shape[0], codes.shape[1] * 4)


def dequantize(codes, scales):
    levels = unpack_levels(codes).astype(jnp.float32) - 8.0
    spread = jnp.repeat(scales.astype(jnp.float32), GROUP, axis=0)
    return (levels * spread).astype(jnp.bfloat16)


def local(
    teacher_in,
    codes,
    scales,
    teacher_resid,
    teacher_gain,
    projector,
    routes,
    student_in,
    queries,
    keys,
    segments,
    value_weight,
):
    dp_count = lax.axis_size("dp")
    fsdp_count = lax.axis_size("fsdp")
    tensor_count = lax.axis_size("tensor")
    dp_place = lax.axis_index("dp")
    fsdp_place = lax.axis_index("fsdp")
    tensor_place = lax.axis_index("tensor")
    weight = dequantize(codes, scales)
    partial_value = jnp.dot(teacher_in, weight, preferred_element_type=jnp.float32)
    teacher_rows = partial_value.shape[0]
    shaped = partial_value.reshape(teacher_rows, fsdp_count, partial_value.shape[1] // fsdp_count)
    summed = lax.psum(shaped.astype(jnp.bfloat16), "tensor").astype(jnp.float32)
    slab_width = shaped.shape[2] // tensor_count
    my_columns = lax.dynamic_slice_in_dim(summed, tensor_place * slab_width, slab_width, 2)
    hidden = my_columns + teacher_resid.astype(jnp.float32)
    row_power = lax.psum(jnp.sum(hidden * hidden, axis=(1, 2)), "tensor")
    row_scale = lax.rsqrt(row_power / HT + EPS)
    normed = (hidden * row_scale[:, None, None] * teacher_gain.astype(jnp.float32)[None]).astype(
        jnp.bfloat16
    )
    query_width = queries.shape[1]
    picked = normed
    target_part = jnp.einsum(
        "rkc,kcq->rq",
        picked,
        lax.all_gather(projector, "fsdp", axis=0, tiled=True),
        preferred_element_type=jnp.float32,
    )
    target = lax.psum(target_part.astype(jnp.bfloat16), "tensor")
    route_grid = routes[:, 0].reshape(dp_count, fsdp_count, tensor_count, -1)
    blocks_dev = route_grid.shape[3]
    share_rows = teacher_rows // tensor_count
    block_rows = share_rows // blocks_dev
    my_target = lax.dynamic_slice_in_dim(target, tensor_place * share_rows, share_rows, 0).reshape(
        blocks_dev, block_rows, query_width
    )
    own_routes = lax.dynamic_slice(
        route_grid, (dp_place, fsdp_place, tensor_place, 0), (1, 1, 1, blocks_dev)
    ).reshape(blocks_dev)
    group_iota = jnp.arange(dp_count, dtype=jnp.int32)
    select = (own_routes[None, :] == group_iota[:, None]).astype(jnp.bfloat16)
    outgoing = jnp.einsum(
        "gj,jrq->grq", select, my_target, preferred_element_type=jnp.float32
    ).astype(jnp.bfloat16)
    incoming = lax.all_to_all(outgoing, "dp", split_axis=0, concat_axis=0, tiled=True)
    senders = lax.dynamic_slice(
        route_grid, (0, fsdp_place, tensor_place, 0), (dp_count, 1, 1, blocks_dev)
    ).reshape(dp_count, blocks_dev)
    arrived = jnp.any(senders == dp_place, axis=1).astype(jnp.float32)
    student_rows = student_in.shape[0]
    lead_rows = dp_count * block_rows
    student_target = jnp.concatenate(
        [
            incoming.reshape(lead_rows, query_width),
            jnp.zeros((student_rows - lead_rows, query_width), jnp.bfloat16),
        ],
        axis=0,
    )
    row_mask = jnp.concatenate(
        [jnp.repeat(arrived, block_rows), jnp.zeros((student_rows - lead_rows,), jnp.float32)]
    )
    value_width = keys.shape[1]
    picked = student_in
    values = jnp.dot(
        picked,
        lax.all_gather(value_weight, ("fsdp", "tensor"), axis=0, tiled=True),
        preferred_element_type=jnp.float32,
    ).astype(jnp.bfloat16)
    kv_heads = value_width // HEAD
    members = query_width // value_width
    query_heads = queries.reshape(student_rows, kv_heads, members, HEAD)
    key_heads = keys.reshape(student_rows, kv_heads, HEAD)
    value_heads = values.reshape(student_rows, kv_heads, HEAD)
    scores = jnp.einsum(
        "sgkd,tgd->gkst", query_heads, key_heads, preferred_element_type=jnp.float32
    ) * HEAD ** (-0.5)
    places = jnp.arange(student_rows, dtype=jnp.int32)
    allowed = (segments[:, None] == segments[None, :]) & (places[:, None] >= places[None, :])
    scores = jnp.where(allowed, scores, -1e30)
    highest = jnp.max(scores, axis=-1, keepdims=True)
    weights = jnp.exp(scores - highest)
    probs = (weights / jnp.sum(weights, axis=-1, keepdims=True)).astype(jnp.bfloat16)
    attended = jnp.einsum(
        "gkst,tgd->sgkd", probs, value_heads, preferred_element_type=jnp.float32
    ).reshape(student_rows, query_width)
    diff = attended - student_target.astype(jnp.float32)
    masked = diff * row_mask[:, None]
    loss_term = jnp.sum(masked * diff)
    grad_att = (2.0 * masked / query_width).astype(jnp.bfloat16)
    grad_heads = grad_att.reshape(student_rows, kv_heads, members, HEAD)
    grad_values = (
        jnp.einsum("gkst,sgkd->tgd", probs, grad_heads, preferred_element_type=jnp.float32)
        .reshape(student_rows, value_width)
        .astype(jnp.bfloat16)
    )
    picked = student_in
    grad_share = lax.psum_scatter(
        lax.dot_general(
            picked, grad_values, (((0,), (0,)), ((), ())), preferred_element_type=jnp.float32
        ),
        ("fsdp", "tensor"),
        scatter_dimension=0,
        tiled=True,
    )
    grad_value = lax.psum(grad_share, "dp")
    total_rows = teacher_rows * dp_count * fsdp_count
    loss = lax.psum(loss_term, ("dp", "fsdp", "tensor")) / (total_rows * query_width)
    return (loss, grad_value)


def solution(mesh):
    return jax.shard_map(
        local,
        mesh=mesh,
        in_specs=(
            P(("dp", "fsdp"), "tensor"),
            P("tensor", None),
            P("tensor", None),
            P(("dp", "fsdp"), None, "tensor"),
            P(None, "tensor"),
            P("fsdp", "tensor", None),
            P(),
            P(("dp", "fsdp", "tensor"), None),
            P(("dp", "fsdp", "tensor"), None),
            P(("dp", "fsdp", "tensor"), None),
            P(("dp", "fsdp", "tensor")),
            P(("fsdp", "tensor"), None),
        ),
        out_specs=(P(), P(("fsdp", "tensor"), None)),
        check_vma=False,
    )
```

profile of v0, /device:TPU:1, one launch (start us, length us, event | category | flops | bytes accessed | tf_op | source)
XLA Modules:
  0.0 537.6 jit_solution(12509442035102224991)
XLA Ops:
  8.0 0.0 all-reduce.7.cloned.1.call-start
  8.1 2.7 and_bitcast_fusion.3
  10.8 3.8 fusion.2
  14.6 10.2 %copy.47 = f32[512,1024,4]{0,2,1:T(4,128)} copy(f32[512,1024,4]{1,0,2:T(8,128)} %fusion.2) | data formatting | bytes 16777216 | tf_op jit(solution)/shard_map/sub | solution.py:23
  24.8 10.0 %sub.20 = f32[512,4096]{0,1:T(8,128)} reshape(f32[512,1024,4]{0,2,1:T(4,128)} %copy.47) | data formatting | bytes 16777216 | tf_op jit(solution)/shard_map/sub | solution.py:23
  34.8 0.4 copy.48
  35.3 9.5 %broadcast_in_dim.12 = f32[4,128,4096]{1,0,2:T(4,128)S(1)} broadcast(f32[4,4096]{0,1:T(8,128)S(1)} %copy.48), dimensions={0,2} | broadcast | bytes 8454144 | tf_op jit(solution)/shard_map/broadcast_in_dim | solution.py:24
  44.8 2.6 convolution_convert_fusion
  47.4 0.0 all-gather.3.cloned.1.call-start
  47.5 0.5 all-gather.3.cloned.1.call-update
  48.0 0.0 all-reduce.9.cloned.1.call-start
  48.1 0.5 broadcast.36
  48.6 0.7 reduce.4
  49.3 0.3 reshape_squeeze.3
  49.6 0.7 fusion.16
  50.3 85.9 %all-gather = bf16[64,28,256]{2,1,0:T(8,128)(2,1)S(1)} all-gather(bf16[1,28,256]{2,1,0:T(8,128)(2,1)S(1)} %bitcast.91), channel_id=1, replica_groups=mesh['dp'=8,'fsdp'=8,'tensor'=8] {'fsdp','tensor'}, dimensions={0}, use_global_device_ids=true | all-gather | bytes 931840 | tf_op jit(solution)/shard_map/all_gather | solution.py:106
  136.2 43.6 %all-reduce.7.cloned.1.call-done = bf16[256,8,512]{0,2,1:T(8,128)(2,1)} async-done(((bf16[256,8,512]{0,2,1:T(8,128)(2,1)}), bf16[256,8,512]{0,2,1:T(8,128)(2,1)}) %all-reduce.7.cloned.1.call-update) | async-done | bytes 2097168 | tf_op jit(solution)/shard_map/psum | solution.py:52
  179.8 1.1 multiply_reduce_fusion
  180.8 14.6 %psum.36 = f32[256]{0:T(256)S(1)} all-reduce(f32[256]{0:T(256)S(1)} %multiply_reduce_fusion), channel_id=1, replica_groups=mesh['dp'=8,'fsdp'=8,'tensor'=8] {'tensor'}, use_global_device_ids=true, to_apply=%region_4.0 | all-reduce | flops 256 | bytes 2048 | tf_op jit(solution)/shard_map/psum | solution.py:56
  195.5 3.4 fusion.5
  198.9 1.3 copy.43
  200.3 1.1 reshape.60
  201.4 0.2 copy-done.4
  201.6 3.9 fusion.33
  205.4 2.4 divide_convert_fusion
  207.8 72.6 %all-reduce.9.cloned.1.call-done = bf16[256,1792]{1,0:T(8,128)(2,1)} async-done(((bf16[256,1792]{1,0:T(8,128)(2,1)}), bf16[256,1792]{1,0:T(8,128)(2,1)}) %all-reduce.9.cloned.1.call-update) | async-done | bytes 917520 | tf_op jit(solution)/shard_map/psum | solution.py:69
  280.4 0.9 dynamic-slice_bitcast_fusion
  281.3 0.3 convolution_convert_fusion.1
  281.7 0.7 copy.50
  282.4 6.3 %all-to-all-start = ((bf16[8,8,1792]{2,1,0:T(8,128)(2,1)}), bf16[8,8,1792]{2,1,0:T(8,128)(2,1)S(1)}, u32[]{:S(2)}, u32[]{:S(2)}) async-start(bf16[8,8,1792]{2,1,0:T(8,128)(2,1)} %copy.50), calls=%async_computation | async-start | bytes 458752 | tf_op jit(solution)/shard_map/all_to_all | solution.py:85
  288.7 0.0 all-reduce.11.cloned.1.call-start
  288.8 1.7 convolution_convert_fusion.2
  290.5 0.2 compare_reduce_fusion
  290.7 0.1 broadcast_in_dim.15
  290.8 0.1 reshape.57
  290.9 1.7 fusion.38
  292.5 2.8 copy.51
  295.3 2.5 all-to-all-done
  297.8 3.3 fusion.7
  301.1 2.2 copy.52
  303.4 1.9 fusion.11
  305.3 1.6 convolution_bitcast_fusion
  307.0 1.3 dynamic-slice
  308.9 100.7 %psum.38 = f32[]{:T(128)} all-reduce(f32[]{:T(128)} %get-tuple-element.15), channel_id=1, replica_groups=mesh['dp'=8,'fsdp'=8,'tensor'=8] {'dp','fsdp','tensor'}, use_global_device_ids=true, to_apply=%region_8.9 | all-reduce | flops 1 | bytes 8 | tf_op jit(solution)/shard_map/psum | solution.py:147
  410.3 93.6 %all-reduce.11.cloned.1.call-done = f32[1792,256]{0,1:T(8,128)} async-done(((f32[1792,256]{0,1:T(8,128)}), f32[1792,256]{0,1:T(8,128)}) %all-reduce.11.cloned.1.call-update) | async-done | bytes 1835024
  503.8 1.0 constant_dynamic-slice_fusion.1
  504.9 23.8 %psum.39 = f32[28,256]{0,1:T(8,128)S(1)} all-reduce(f32[28,256]{0,1:T(8,128)S(1)} %constant_dynamic-slice_fusion.1), channel_id=1, replica_groups=mesh['dp'=8,'fsdp'=8,'tensor'=8] {'dp'}, use_global_device_ids=true, to_apply=%region_10.11 | all-reduce | flops 7168 | bytes 57344 | tf_op jit(solution)/shard_map/psum | solution.py:145
  528.6 0.7 copy.54
  (33 shorter events, 0.2 us)
Async XLA Ops:
  8.0 280.8 %copy-start = (bf16[256,1792]{1,0:T(8,128)(2,1)S(1)}, bf16[256,1792]{1,0:T(8,128)(2,1)}, u32[]{:S(2)}) copy-start(bf16[256,1792]{1,0:T(8,128)(2,1)} %param.19) | copy-start | bytes 2752516
  8.0 171.8 %all-reduce.7.cloned.1.call-start = ((), (), s32[]{:S(2)}) async-start(), calls=%async_computation.1 | async-start | bytes 4194304 | tf_op jit(solution)/shard_map/psum | solution.py:52
  24.8 10.0 %copy-start.7 = (bf16[4,4096]{1,0:T(4,128)(2,1)S(1)}, bf16[4,4096]{1,0:T(4,128)(2,1)}, u32[]{:S(2)}) copy-start(bf16[4,4096]{1,0:T(4,128)(2,1)} %param.14) | copy-start | bytes 98308
  35.3 9.5 %copy-start.1 = (f32[512,4096]{0,1:T(8,128)S(1)}, f32[512,4096]{0,1:T(8,128)}, u32[]{:S(2)}) copy-start(f32[512,4096]{0,1:T(8,128)} %sub.20) | copy-start | bytes 25165828
  35.3 9.5 %copy-start.5 = (bf16[256,512]{1,0:T(8,128)(2,1)S(1)}, bf16[256,512]{1,0:T(8,128)(2,1)}, u32[]{:S(2)}) copy-start(bf16[256,512]{1,0:T(8,128)(2,1)} %param.12) | copy-start | bytes 786436
  47.4 0.7 copy-start.11
  47.4 1.2 copy-start.9
  47.4 2.2 copy-start.10
  47.4 2.9 copy-start.8
  47.4 132.4 %copy-start.2 = (bf16[256,8,64]{0,2,1:T(8,128)(2,1)S(1)}, bf16[256,8,64]{0,2,1:T(8,128)(2,1)}, u32[]{:S(2)}) copy-start(bf16[256,8,64]{0,2,1:T(8,128)(2,1)} %param.15) | copy-start | bytes 786436
  47.4 148.0 %all-gather.3.cloned.1.call-start = ((), (), s32[]{:S(2)}) async-start(), calls=%async_computation.2 | async-start | bytes 2064384 | tf_op jit(solution)/shard_map/all_gather | solution.py:66
  48.0 232.4 %all-reduce.9.cloned.1.call-start = ((), (), s32[]{:S(2)}) async-start(), calls=%async_computation.3 | async-start | bytes 1835008 | tf_op jit(solution)/shard_map/psum | solution.py:69
  195.5 3.5 copy-start.3
  198.9 1.4 copy-start.6
  200.3 1.3 copy-start.4
  282.4 15.4 %all-to-all-start = ((bf16[8,8,1792]{2,1,0:T(8,128)(2,1)}), bf16[8,8,1792]{2,1,0:T(8,128)(2,1)S(1)}, u32[]{:S(2)}, u32[]{:S(2)}) async-start(bf16[8,8,1792]{2,1,0:T(8,128)(2,1)} %copy.50), calls=%async_computation | async-start | bytes 458752 | tf_op jit(solution)/shard_map/all_to_all | solution.py:85
  288.7 215.1 %all-reduce.11.cloned.1.call-start = ((), (), s32[]{:S(2)}) async-start(), calls=%async_computation.4 | async-start | bytes 3670016
Sparse Core Ops, SparseCore 0:
  47.6 132.1 all-reduce.6
  199.0 81.3 all-reduce.8
  307.1 196.7 all-reduce.10
Sparse Core Ops, SparseCore 1:
  50.0 76.4 all-gather.2
where the time goes:
time: 547 us; the launch traced here: 538 us
  blocking collectives  225 us (41%)
  waiting for transfers between devices  213 us (39%)
  local copies, waits for them, and re-layouts  43.4 us (8%)
  between operations  17.8 us (3%)
  matrix products  17.1 us (3%)
  other arithmetic  15 us (3%)
  starting transfers between devices  6.5 us (1%)
    psum x1, blocking collectives, local(): lax.psum(loss_term, ('dp', 'fsdp', 'tensor')) / (total_rows * query_width)  101 us
    unnamed x5, waiting for transfers between devices  94.1 us
    all_gather x1, blocking collectives, local(): lax.all_gather(value_weight, ('fsdp', 'tensor'), axis=0, tiled=True)  85.9 us
    psum x1, waiting for transfers between devices, local(): target = lax.psum(target_part.astype(jnp.bfloat16), 'tensor')  72.6 us
    psum x1, waiting for transfers between devices, local(): summed = lax.psum(shaped.astype(jnp.bfloat16), 'tensor').astype(jnp.float32)  43.6 us
    psum x1, blocking collectives, local(): grad_value = lax.psum(grad_share, 'dp')  23.8 us
    sub x2, local copies, waits for them, and re-layouts, dequantize(): levels = unpack_levels(codes).astype(jnp.float32) - 8.0  20.2 us
    psum x1, blocking collectives, local(): row_power = lax.psum(jnp.sum(hidden * hidden, axis=(1, 2)), 'tensor')  14.6 us
  transfers between devices with their start and end apart: 5, of which 4 were waited for; matrix products, arithmetic and copies ran while one was open for 4% of the time, Pallas kernels for 0%

commit v1 on v0

v1 whole, which is shorter than its diff:
```python
import functools
from types import SimpleNamespace

import jax
import jax.numpy as jnp
from jax import lax
from jax.experimental import pallas as pl
from jax.experimental.pallas import tpu as pltpu
from jax.sharding import PartitionSpec as P

HT = 4096
GROUP = 128
HEAD = 128
EPS = 1e-06
F32, BF16 = jnp.float32, jnp.bfloat16
MESH = pl.DeviceIdType.MESH

N = 8
ZH = 4
LEAD = 64
QW = 1792
KVW = 256
WIDE = QW + 128
HALF = QW // 2
TAIL = 16


def scratch_spec():
    dma, vmem = pltpu.SemaphoreType.DMA, pltpu.VMEM
    return dict(
        codes_sib=vmem((512, 1024), jnp.int32),
        perm=vmem((8, 1024, 128), jnp.int32),
        xb=vmem((2, 4, 32, 512), BF16),
        resb=vmem((2, 4, 32, 512), BF16),
        gainb=vmem((2, 8, 512), F32),
        scraw=vmem((2, 64, 512), F32),
        scp=vmem((2, 64, 512), F32),
        spread=vmem((512, 512), BF16),
        wbuf=vmem((1024, 1024), BF16),
        part=vmem((ZH, 128, 1024), BF16),
        relay=vmem((2, 64, 1024), BF16),
        near=vmem((2, 64, 1024), BF16),
        added=vmem((2, 64, 1024), BF16),
        summed=vmem((2, 64, 1024), BF16),
        proj=vmem((2, 8, 64, QW), BF16),
        pbuf=vmem((ZH, 32, WIDE), BF16),
        relay4=vmem((2, 16, WIDE), BF16),
        near4=vmem((2, 16, WIDE), BF16),
        added4=vmem((2, 16, WIDE), BF16),
        summed4=vmem((2, 16, WIDE), BF16),
        osend=vmem((8, 16, HALF), BF16),
        trecv=vmem((8, 16, HALF), BF16),
        q=vmem((LEAD, QW), BF16),
        k=vmem((LEAD, KVW), BF16),
        sb=vmem((8, LEAD, KVW), BF16),
        vw=vmem((8, 32, KVW), BF16),
        pvs=vmem((8, LEAD, KVW), BF16),
        pvr=vmem((8, LEAD, KVW), BF16),
        probs=vmem((2, 7 * LEAD, LEAD), BF16),
        att=vmem((2, 7 * LEAD, HEAD), F32),
        g1=vmem((8, LEAD + TAIL, KVW), BF16),
        g2s=vmem((8, 32 + TAIL, KVW), BF16),
        g2r=vmem((8, 32 + TAIL, KVW), BF16),
        g3=vmem((8, 32 + TAIL, KVW), BF16),
        qk_sem=dma((2,)),
        sib_s=dma((5,)),
        sib_r=dma((5,)),
        p_s=dma((10,)),
        p_r=dma((8, 2)),
        psib_r=dma((1,)),
        t1_s=dma((6,)),
        t1_r=dma((6,)),
        t4_s=dma((6,)),
        t4_r=dma((6,)),
        stu_s=dma((8,)),
        stu_r=dma((8,)),
        vw_s=dma((8,)),
        vw_r=dma((8,)),
        pv_s=dma((8,)),
        pv_r=dma((8,)),
        t5_s=dma((8,)),
        t5_r=dma((8,)),
        g1_s=dma((8,)),
        g1_r=dma((8,)),
        g2_s=dma((8,)),
        g2_r=dma((8,)),
        g3_s=dma((8,)),
        g3_r=dma((8,)),
    )


def dot(a, b, dims=((1,), (0,))):
    return lax.dot_general(a, b, (dims, ((), ())), preferred_element_type=F32)


def remote(src, dst, send, recv, **device):
    return pltpu.make_async_remote_copy(
        src_ref=src,
        dst_ref=dst,
        send_sem=send,
        recv_sem=recv,
        device_id=device,
        device_id_type=MESH,
    )


class Exchange:
    def __init__(self, axis, me, src, dst, send, recv):
        self.axis, self.me, self.src, self.dst = axis, me, src, dst
        self.send, self.recv = send, recv

    def each(self, act):
        def body(step, carry):
            act(lax.rem(self.me + step, N))
            return carry

        lax.fori_loop(1, N, body, 0)

    def copy(self, peer, slot):
        return remote(
            self.src(peer),
            self.dst.at[slot],
            self.send.at[peer],
            self.recv.at[slot],
            **{self.axis: peer},
        )

    def start(self):
        self.each(lambda peer: self.copy(peer, self.me).start())

    def wait_recv(self):
        self.each(lambda peer: self.copy(peer, peer).wait_recv())

    def wait_send(self):
        self.each(lambda peer: self.copy(peer, self.me).wait_send())


def split_sum(total):
    high = total.astype(BF16).astype(F32)
    lane = lax.broadcasted_iota(jnp.int32, (total.shape[0], 128), 1)
    return jnp.where(lane == 0, high, jnp.where(lane == 1, total - high, 0.0)).astype(BF16)


def split_scalar(value):
    row = lax.broadcasted_iota(jnp.int32, (TAIL, KVW), 0)
    lane = lax.broadcasted_iota(jnp.int32, (TAIL, KVW), 1)
    spread = jnp.full((TAIL, KVW), value, F32)
    high = spread.astype(BF16).astype(F32)
    rest = spread - high
    middle = rest.astype(BF16).astype(F32)
    low = rest - middle
    picked = jnp.where(lane == 0, high, jnp.where(lane == 1, middle, jnp.where(lane == 2, low, 0.0)))
    return jnp.where(row == 0, picked, 0.0).astype(BF16)


def add_wide(a, b):
    a, b = a.astype(F32), b.astype(F32)
    power = jnp.sum(a[:, QW:], axis=1, keepdims=True) + jnp.sum(b[:, QW:], axis=1, keepdims=True)
    return (a[:, :QW] + b[:, :QW]).astype(BF16), split_sum(power)


def kernel(
    total_count,
    names,
    x_ref,
    codes_ref,
    scales_ref,
    resid_ref,
    gain_ref,
    proj_ref,
    routes_ref,
    stu_ref,
    allow_ref,
    vw_ref,
    q_ref,
    k_ref,
    loss_ref,
    grad_ref,
    *scratch,
):
    m = SimpleNamespace(**dict(zip(names, scratch)))
    d, f, t = lax.axis_index("dp"), lax.axis_index("fsdp"), lax.axis_index("tensor")
    zh, c = lax.div(t, 2), lax.rem(t, 2)
    other = 1 - c
    sib = t + 1 - 2 * c
    zp, zm = lax.rem(t + 2, N), lax.rem(t + 6, N)
    fz = f + 1 - 2 * lax.rem(f, 2)
    xp, xm = lax.rem(f + 2, N), lax.rem(f + 6, N)
    xpz, xmz = xp + 1 - 2 * lax.rem(xp, 2), xm + 1 - 2 * lax.rem(xm, 2)
    xf = lax.rem(f + 4, N)
    xfz = xf + 1 - 2 * lax.rem(xf, 2)

    barrier = pltpu.get_barrier_semaphore()

    def greet(step, carry):
        for axis, me in (("tensor", t), ("fsdp", f), ("dp", d)):
            pl.semaphore_signal(
                barrier, inc=1, device_id={axis: lax.rem(me + step, N)}, device_id_type=MESH
            )
        return carry

    lax.fori_loop(1, N, greet, 0)
    pl.semaphore_wait(barrier, 3 * (N - 1))

    sib_copies = [
        remote(codes_ref, m.codes_sib, m.sib_s.at[0], m.sib_r.at[0], tensor=sib),
        remote(x_ref.at[:, other], m.xb.at[c], m.sib_s.at[1], m.sib_r.at[1], tensor=sib),
        remote(scales_ref, m.scraw.at[c], m.sib_s.at[2], m.sib_r.at[2], tensor=sib),
        remote(resid_ref.at[:, other], m.resb.at[c], m.sib_s.at[3], m.sib_r.at[3], tensor=sib),
        remote(gain_ref, m.gainb.at[c], m.sib_s.at[4], m.sib_r.at[4], tensor=sib),
    ]
    sib_waits = [
        remote(codes_ref, m.codes_sib, m.sib_s.at[0], m.sib_r.at[0], tensor=sib),
        remote(x_ref.at[:, other], m.xb.at[other], m.sib_s.at[1], m.sib_r.at[1], tensor=sib),
        remote(scales_ref, m.scraw.at[other], m.sib_s.at[2], m.sib_r.at[2], tensor=sib),
        remote(resid_ref.at[:, other], m.resb.at[other], m.sib_s.at[3], m.sib_r.at[3], tensor=sib),
        remote(gain_ref, m.gainb.at[other], m.sib_s.at[4], m.sib_r.at[4], tensor=sib),
    ]
    for copy in sib_copies:
        copy.start()

    def block(owner):
        return m.proj.at[c, owner]

    def half_block(owner, half):
        return m.proj.at[c, owner, pl.ds(32 * half, 32)]

    to_z = remote(proj_ref, block(f), m.p_s.at[0], m.p_r.at[f, 0], fsdp=fz)
    to_x = [
        remote(proj_ref, block(f), m.p_s.at[1], m.p_r.at[f, 0], fsdp=xp),
        remote(proj_ref, block(f), m.p_s.at[2], m.p_r.at[f, 0], fsdp=xm),
    ]
    to_xz = [
        remote(block(fz), block(fz), m.p_s.at[3], m.p_r.at[fz, 0], fsdp=xp),
        remote(block(fz), block(fz), m.p_s.at[4], m.p_r.at[fz, 0], fsdp=xm),
    ]
    forward = [
        remote(half_block(xm, 0), half_block(xm, 0), m.p_s.at[5], m.p_r.at[xm, 0], fsdp=xp),
        remote(half_block(xp, 1), half_block(xp, 1), m.p_s.at[6], m.p_r.at[xp, 1], fsdp=xm),
        remote(half_block(xmz, 0), half_block(xmz, 0), m.p_s.at[7], m.p_r.at[xmz, 0], fsdp=xp),
        remote(half_block(xpz, 1), half_block(xpz, 1), m.p_s.at[8], m.p_r.at[xpz, 1], fsdp=xm),
    ]

    def arrived(owner):
        return remote(proj_ref, block(owner), m.p_s.at[0], m.p_r.at[owner, 0], fsdp=fz)

    def arrived_half(owner, half):
        return remote(
            half_block(owner, half), half_block(owner, half), m.p_s.at[5], m.p_r.at[owner, half], fsdp=xp
        )

    to_sib = remote(m.proj.at[c], m.proj.at[c], m.p_s.at[9], m.psib_r.at[0], tensor=sib)
    from_sib = remote(m.proj.at[other], m.proj.at[other], m.p_s.at[9], m.psib_r.at[0], tensor=sib)
    to_z.start()
    for copy in to_x:
        copy.start()

    students = Exchange("fsdp", f, lambda peer: stu_ref.at[peer], m.sb, m.stu_s, m.stu_r)
    value_rows = Exchange("tensor", t, lambda peer: vw_ref, m.vw, m.vw_s, m.vw_r)
    value_parts = Exchange("fsdp", f, lambda peer: m.pvs.at[peer], m.pvr, m.pv_s, m.pv_r)
    targets = Exchange("dp", d, lambda peer: m.osend.at[peer], m.trecv, m.t5_s, m.t5_r)
    grads1 = Exchange("fsdp", f, lambda peer: m.g1.at[f], m.g1, m.g1_s, m.g1_r)
    grads2 = Exchange("tensor", t, lambda peer: m.g2s.at[peer], m.g2r, m.g2_s, m.g2_r)
    grads3 = Exchange("dp", d, lambda peer: m.g3.at[d], m.g3, m.g3_s, m.g3_r)
    students.start()
    value_rows.start()
    queries_in = pltpu.make_async_copy(q_ref.at[pl.ds(0, LEAD)], m.q, m.qk_sem.at[0])
    keys_in = pltpu.make_async_copy(k_ref.at[pl.ds(0, LEAD)], m.k, m.qk_sem.at[1])
    queries_in.start()
    keys_in.start()

    for b in range(4):
        m.xb[c, b] = x_ref[b, c]
        m.resb[c, b] = resid_ref[b, c]
    m.gainb[c] = gain_ref[...]
    m.scraw[c] = scales_ref[...]
    m.proj[c, f] = proj_ref[...]
    m.sb[f] = stu_ref[f]
    m.vw[t] = vw_ref[...]

    row = lax.broadcasted_iota(jnp.int32, (512, 512), 0)
    col = lax.broadcasted_iota(jnp.int32, (512, 512), 1)
    own_order = ((row >> 4) & 7) * 64 + (row & 15) * 4 + (row >> 7)
    m.spread[...] = jnp.where(own_order == col, 1.0, 0.0).astype(BF16)

    def shuffle(src, slot):
        lane = lax.broadcasted_iota(jnp.int32, (32, 128), 1)

        def body(i, carry):
            at = pl.multiple_of(i * 32, 32)
            a = [src[pl.ds(at, 32), j * 128 : (j + 1) * 128] for j in range(8)]
            for step in (4, 2, 1):
                upper = (lane & (16 * step)) != 0
                new = list(a)
                for j in range(8):
                    if j & step == 0:
                        low, high = a[j], a[j + step]
                        new[j] = jnp.where(upper, pltpu.roll(high, 16 * step, 1), low)
                        new[j + step] = jnp.where(upper, high, pltpu.roll(low, 128 - 16 * step, 1))
                a = new
            for j in range(8):
                m.perm[j, pl.ds(pl.multiple_of(slot * 512 + i * 32, 32), 32), :] = a[j]
            return carry

        lax.fori_loop(0, 16, body, 0)

    shuffle(codes_ref, c)
    for copy in sib_waits:
        copy.wait_recv()
    shuffle(m.codes_sib, other)
    for slot in range(2):
        m.scp[slot] = dot(m.scraw[slot].astype(BF16), m.spread[...], ((1,), (1,)))

    def partial(r):
        z = lax.rem(zh + r, ZH)

        def body(i, carry):
            s, src = lax.div(i, 2), lax.rem(i, 2)
            slice_at = 2 * z + s
            sc = m.scp[src, pl.ds(pl.multiple_of(slice_at * 8, 8), 8), :]
            for g in range(4):
                at = pl.multiple_of(src * 512 + g * GROUP, GROUP)
                words = m.perm[slice_at, pl.ds(at, GROUP), :]
                for level in range(4):
                    value = (lax.shift_right_logical(words, 4 * level) & 15).astype(F32) - 8.0
                    value = value * sc[g : g + 1, level * 128 : (level + 1) * 128]
                    lanes = pl.ds(pl.multiple_of(s * 512 + level * 128, 128), 128)
                    m.wbuf[pl.ds(at, GROUP), lanes] = value.astype(BF16)
            return carry

        lax.fori_loop(0, 4, body, 0)
        x0 = m.xb[0].reshape(128, 512)
        x1 = m.xb[1].reshape(128, 512)
        for s in range(2):
            lanes = slice(s * 512, (s + 1) * 512)
            acc = dot(x0, m.wbuf[0:512, lanes]) + dot(x1, m.wbuf[512:1024, lanes])
            m.part[r, :, lanes] = dot(acc.astype(BF16), m.spread[...]).astype(BF16)

    def ring(src, relay, near, added, summed, send, recv, half):
        low, high = pl.ds(0, half), pl.ds(half, half)
        far = [
            remote(src(2, low), relay.at[0], send.at[0], recv.at[0], tensor=zp),
            remote(src(2, high), relay.at[1], send.at[1], recv.at[1], tensor=zm),
        ]
        direct = [
            remote(src(1, high), near.at[0], send.at[2], recv.at[2], tensor=zp),
            remote(src(3, low), near.at[1], send.at[3], recv.at[3], tensor=zm),
        ]
        sums = [
            remote(added.at[0], summed.at[0], send.at[4], recv.at[4], tensor=zp),
            remote(added.at[1], summed.at[1], send.at[5], recv.at[5], tensor=zm),
        ]
        return far, direct, sums

    far, direct, sums = ring(
        lambda r, rows: m.part.at[r, rows], m.relay, m.near, m.added, m.summed, m.t1_s, m.t1_r, 64
    )
    partial(2)
    far[0].start()
    far[1].start()
    arrived(fz).wait_recv()
    for copy in to_xz:
        copy.start()
    partial(1)
    direct[0].start()
    partial(3)
    direct[1].start()

    students.wait_recv()
    value_rows.wait_recv()
    rows_of_value = m.vw[...].reshape(8 * 32, KVW)
    value_part = dot(m.sb[...].reshape(8 * LEAD, KVW), rows_of_value)
    m.pvs[...] = value_part.reshape(8, LEAD, KVW).astype(BF16)
    m.pvr[f] = m.pvs[f]
    value_parts.start()
    far[0].wait_recv()
    m.added[0] = (m.part[1, 0:64].astype(F32) + m.relay[0].astype(F32)).astype(BF16)
    sums[0].start()
    far[1].wait_recv()
    m.added[1] = (m.part[3, 64:128].astype(F32) + m.relay[1].astype(F32)).astype(BF16)
    sums[1].start()
    partial(0)

    for owner in (xm, xp, xmz, xpz):
        arrived(owner).wait_recv()
    for copy in forward:
        copy.start()

    queries_in.wait()
    keys_in.wait()
    allow = jnp.concatenate([allow_ref[...]] * 7, axis=0)
    for g in range(2):
        heads = [m.q[:, (g * 7 + h) * HEAD : (g * 7 + h + 1) * HEAD] for h in range(7)]
        scores = dot(jnp.concatenate(heads, axis=0), m.k[:, g * HEAD : (g + 1) * HEAD], ((1,), (1,)))
        scores = jnp.where(allow > 0.0, scores * HEAD ** (-0.5), -1e30)
        weights = jnp.exp(scores - jnp.max(scores, axis=1, keepdims=True))
        m.probs[g] = (weights / jnp.sum(weights, axis=1, keepdims=True)).astype(BF16)
    value_parts.wait_recv()
    values = m.pvr[0].astype(F32)
    for j in range(1, 8):
        values = values + m.pvr[j].astype(F32)
    values = values.astype(BF16)
    for g in range(2):
        m.att[g] = dot(m.probs[g], values[:, g * HEAD : (g + 1) * HEAD])

    for owner in (xf, xfz):
        for half in range(2):
            arrived_half(owner, half).wait_recv()
    to_sib.start()

    for copy in direct:
        copy.wait_recv()
    for copy in sums:
        copy.wait_recv()
    from_sib.wait_recv()
    lower = m.part[0, 0:64].astype(F32) + m.summed[0].astype(F32) + m.near[1].astype(F32)
    upper = m.part[0, 64:128].astype(F32) + m.near[0].astype(F32) + m.summed[1].astype(F32)
    out = jnp.concatenate([lower, upper], axis=0)
    power = jnp.zeros((128, 1), F32)
    scaled = []
    for s in range(2):
        hidden = out[:, s * 512 : (s + 1) * 512] + m.resb[s].reshape(128, 512).astype(F32)
        power = power + jnp.sum(hidden * hidden, axis=1, keepdims=True)
        scaled.append((hidden * m.gainb[s, 0:1, :]).astype(BF16))
    m.pbuf[:, :, QW:] = split_sum(power).reshape(ZH, 32, 128)
    for j in range(7):
        lanes = slice(j * 256, (j + 1) * 256)
        acc = dot(scaled[0], m.proj[0, :, :, lanes].reshape(512, 256))
        acc = acc + dot(scaled[1], m.proj[1, :, :, lanes].reshape(512, 256))
        m.pbuf[:, :, lanes] = acc.astype(BF16).reshape(ZH, 32, 256)

    far4, direct4, sums4 = ring(
        lambda r, rows: m.pbuf.at[lax.rem(zh + r, ZH), rows],
        m.relay4,
        m.near4,
        m.added4,
        m.summed4,
        m.t4_s,
        m.t4_r,
        16,
    )
    for copy in far4 + direct4:
        copy.start()

    row = lax.broadcasted_iota(jnp.int32, (64, 32), 0)
    col = lax.broadcasted_iota(jnp.int32, (64, 32), 1)
    place = ((d * N + f) * N + t) * 4
    wanted = jnp.full((64, 32), -1, jnp.int32)
    for j in range(4):
        wanted = jnp.where((col >> 3) == j, routes_ref[place + j], wanted)
    select = jnp.where(((row >> 3) == wanted) & ((row & 7) == (col & 7)), 1.0, 0.0).astype(BF16)
    lead = lax.broadcasted_iota(jnp.int32, (LEAD, HEAD), 0) >> 3
    mask = jnp.zeros((LEAD, HEAD), F32)
    for source in range(N):
        for j in range(4):
            hit = routes_ref[((source * N + f) * N + t) * 4 + j] == d
            mask = jnp.where(lead == source, jnp.maximum(mask, jnp.where(hit, 1.0, 0.0)), mask)

    far4[0].wait_recv()
    m.added4[0, :, :QW], m.added4[0, :, QW:] = add_wide(m.pbuf[lax.rem(zh + 1, ZH), 0:16], m.relay4[0])
    sums4[0].start()
    far4[1].wait_recv()
    m.added4[1, :, :QW], m.added4[1, :, QW:] = add_wide(m.pbuf[lax.rem(zh + 3, ZH), 16:32], m.relay4[1])
    sums4[1].start()
    for copy in direct4 + sums4:
        copy.wait_recv()
    own = m.pbuf[zh].astype(F32)
    lower = own[0:16] + m.summed4[0].astype(F32) + m.near4[1].astype(F32)
    upper = own[16:32] + m.near4[0].astype(F32) + m.summed4[1].astype(F32)
    total = jnp.concatenate([lower, upper], axis=0)
    power = jnp.sum(total[:, QW:], axis=1, keepdims=True)
    target = (total[:, :QW] * lax.rsqrt(power / HT + EPS)).astype(BF16)
    routed = dot(select, target)
    m.osend[...] = jnp.concatenate(
        [routed[:, :HALF].reshape(8, 8, HALF), routed[:, HALF:].reshape(8, 8, HALF)], axis=1
    ).astype(BF16)
    m.trecv[d] = m.osend[d]
    targets.start()
    targets.wait_recv()

    received = m.trecv[...].astype(F32)
    halves = [received[:, 0:8].reshape(LEAD, HALF), received[:, 8:16].reshape(LEAD, HALF)]
    lost = jnp.zeros((LEAD, HEAD), F32)
    for g in range(2):
        pieces = []
        for h in range(7):
            wanted = halves[g][:, h * HEAD : (h + 1) * HEAD]
            diff = m.att[g, h * LEAD : (h + 1) * LEAD] - wanted
            masked = diff * mask
            lost = lost + masked * diff
            pieces.append((2.0 * masked / QW).astype(BF16))
        grad = dot(m.probs[g], jnp.concatenate(pieces, axis=0), ((0,), (0,)))
        m.g1[f, 0:LEAD, g * HEAD : (g + 1) * HEAD] = grad.astype(BF16)
    m.g1[f, LEAD:] = split_scalar(jnp.sum(lost))
    grads1.start()
    grads1.wait_recv()
    grad = dot(
        m.sb[...].reshape(8 * LEAD, KVW), m.g1[:, 0:LEAD, :].reshape(8 * LEAD, KVW), ((0,), (0,))
    )
    m.g2s[:, 0:32, :] = grad.reshape(8, 32, KVW).astype(BF16)
    loss_tail = split_scalar(jnp.sum(m.g1[:, LEAD:, :].astype(F32)))
    for j in range(N):
        m.g2s[j, 32:, :] = loss_tail
    m.g2r[t] = m.g2s[t]
    grads2.start()
    grads2.wait_recv()
    m.g3[d, 0:32, :] = jnp.sum(m.g2r[:, 0:32, :].astype(F32), axis=0).astype(BF16)
    m.g3[d, 32:, :] = split_scalar(jnp.sum(m.g2r[:, 32:, :].astype(F32)))
    grads3.start()
    grads3.wait_recv()
    grad_ref[...] = jnp.sum(m.g3[:, 0:32, :].astype(F32), axis=0)
    loss_ref[0, 0] = jnp.sum(m.g3[:, 32:, :].astype(F32)) / total_count

    for copy in sib_copies + [to_z] + to_x + to_xz + forward + [to_sib]:
        copy.wait_send()
    for copy in far + direct + sums + far4 + direct4 + sums4:
        copy.wait_send()
    for exchange in (students, value_rows, value_parts, targets, grads1, grads2, grads3):
        exchange.wait_send()


def local(
    teacher_in,
    codes,
    scales,
    teacher_resid,
    teacher_gain,
    projector,
    routes,
    student_in,
    queries,
    keys,
    segments,
    value_weight,
):
    x = teacher_in.reshape(4, 2, 32, 512)
    resid = teacher_resid.reshape(4, 2, 32, 512)
    gain = jnp.broadcast_to(teacher_gain.astype(F32).reshape(1, 512), (8, 512))
    by_slice = scales.astype(F32).reshape(4, 8, 8, 64).transpose(2, 0, 1, 3).reshape(8, 4, 512)
    by_slice = jnp.pad(by_slice, ((0, 0), (0, 4), (0, 0))).reshape(64, 512)
    lead = student_in[:LEAD].reshape(LEAD, 8, 8, 28)
    lead = jnp.pad(lead, ((0, 0), (0, 0), (0, 0), (0, 4))).transpose(1, 0, 2, 3).reshape(8, LEAD, 256)
    rows = segments[:LEAD]
    places = jnp.arange(LEAD, dtype=jnp.int32)
    allow = (rows[:, None] == rows[None, :]) & (places[:, None] >= places[None, :])
    value_rows = jnp.pad(value_weight, ((0, 4), (0, 0)))
    spec = scratch_spec()
    vmem = pl.BlockSpec(memory_space=pltpu.VMEM)
    smem = pl.BlockSpec(memory_space=pltpu.SMEM)
    anywhere = pl.BlockSpec(memory_space=pl.ANY)
    loss, grad = pl.pallas_call(
        functools.partial(kernel, float(16384 * QW), tuple(spec)),
        out_shape=(
            jax.ShapeDtypeStruct((1, 1), F32),
            jax.ShapeDtypeStruct((32, KVW), F32),
        ),
        in_specs=[vmem] * 6 + [smem] + [vmem] * 3 + [anywhere] * 2,
        out_specs=(smem, vmem),
        scratch_shapes=list(spec.values()),
        compiler_params=pltpu.CompilerParams(
            collective_id=0, has_side_effects=True, vmem_limit_bytes=48 * 1024 * 1024
        ),
        name="distill",
    )(
        x,
        codes,
        by_slice,
        resid,
        gain,
        projector.reshape(64, QW),
        routes.reshape(2048),
        lead,
        allow.astype(F32),
        value_rows,
        queries,
        keys,
    )
    return loss[0, 0], grad[:28]


def solution(mesh):
    return jax.shard_map(
        local,
        mesh=mesh,
        in_specs=(
            P(("dp", "fsdp"), "tensor"),
            P("tensor", None),
            P("tensor", None),
            P(("dp", "fsdp"), None, "tensor"),
            P(None, "tensor"),
            P("fsdp", "tensor", None),
            P(),
            P(("dp", "fsdp", "tensor"), None),
            P(("dp", "fsdp", "tensor"), None),
            P(("dp", "fsdp", "tensor"), None),
            P(("dp", "fsdp", "tensor")),
            P(("fsdp", "tensor"), None),
        ),
        out_specs=(P(), P(("fsdp", "tensor"), None)),
        check_vma=False,
    )
```

time: 547 us -> 117 us (0.21); the launches traced: 538 us -> 116 us
  blocking collectives: 225 us -> 0 us
  waiting for transfers between devices: 213 us -> 0 us
  Pallas kernels: 0 us -> 93 us
  local copies, waits for them, and re-layouts: 43.4 us -> 18.9 us
  matrix products: 17.1 us -> 0 us
  between operations: 17.8 us -> 2.5 us
  other arithmetic: 15 us -> 2.11 us
  starting transfers between devices: 6.5 us -> 0 us
    psum x3 -> x0, blocking collectives: 139 us -> none  [the longest x1 101 us: local(): lax.psum(loss_term, ('dp', 'fsdp', 'tensor')) / (total_rows * query_width)]
    psum x2 -> x0, waiting for transfers between devices: 116 us -> none  [the longest x1 72.6 us: local(): target = lax.psum(target_part.astype(jnp.bfloat16), 'tensor')]
    unnamed x5 -> x0, waiting for transfers between devices: 94.1 us -> none
    pallas_call x0 -> x1, Pallas kernels: none -> 93 us  [local(): pl.pallas_call(functools.partial(kernel, float(16384 * QW), tuple(spec)),...]
    all_gather x1 -> x0, blocking collectives: 85.9 us -> none  [local(): lax.all_gather(value_weight, ('fsdp', 'tensor'), axis=0, tiled=True)]
    sub x2 -> x0, local copies, waits for them, and re-layouts: 20.2 us -> none  [dequantize(): levels = unpack_levels(codes).astype(jnp.float32) - 8.0]
    dot_general x7 -> x0, matrix products: 13.2 us -> none  [the longest x1 3.39 us: local(): jnp.einsum('rkc,kcq->rq', picked, lax.all_gather(projector, 'fsdp', axis=...]
    broadcast_in_dim x2, local copies, waits for them, and re-layouts: 9.56 us -> 0.09 us  [local(): gain = jnp.broadcast_to(teacher_gain.astype(F32).reshape(1, 512), (8, 512))]
  transfers between devices with their start and end apart: 5 -> 0, of which waited for: 4 -> 0; matrix products, arithmetic and copies ran while one was open for 4% -> 0% of each run, Pallas kernels for 0% -> 0%
where the time goes in v1:
time: 117 us; the launch traced here: 116 us
  Pallas kernels  93 us (79%)
  local copies, waits for them, and re-layouts  18.9 us (16%)
  between operations  2.5 us (2%)
  other arithmetic  2.11 us (2%)
    pallas_call x1, Pallas kernels, local(): pl.pallas_call(functools.partial(kernel, float(16384 * QW), tuple(spec)),...  93 us
    unnamed x22, local copies, waits for them, and re-layouts  8.5 us
    reshape x2, local copies, waits for them, and re-layouts, local(): scales.astype(F32).reshape(4, 8, 8, 64).transpose(2, 0, 1, 3)  3.07 us

profile of v1, /device:TPU:1, one launch (start us, length us, event | category | flops | bytes accessed | tf_op | source)
XLA Modules:
  0.0 116.5 jit_solution(9404212750793821391)
XLA Ops:
  0.6 1.0 slice.9
  1.6 0.3 copy.19
  1.9 0.1 reshape.47
  2.0 0.0 slice-start
  2.0 0.0 copy-start.9
  2.0 0.0 copy-start
  2.0 0.0 copy-start.1
  2.0 0.0 copy-start.8
  2.1 0.9 pad.14
  3.0 1.4 %copy.20.stu_ref = bf16[8,64,256]{2,1,0:T(8,128)(2,1)S(1)} copy(bf16[8,64,256]{1,2,0:T(8,128)(2,1)} %bitcast.20) | data formatting | bytes 524288 | tf_op jit(solution)/shard_map/reshape | solution.py:542
  4.4 2.0 %copy.18 = bf16[256,8,64]{2,1,0:T(8,128)(2,1)} copy(bf16[256,8,64]{0,2,1:T(8,128)(2,1)} %param.15) | data formatting | bytes 524288 | tf_op args[3]
  6.4 1.4 %reshape.44.resid_ref = bf16[4,2,32,512]{3,2,1,0:T(8,128)(2,1)S(1)} reshape(bf16[256,8,64]{2,1,0:T(8,128)(2,1)} %copy.18) | data formatting | bytes 524288 | tf_op jit(solution)/shard_map/reshape | solution.py:537
  7.8 1.5 %reshape.40 = bf16[4,8,8,64]{3,2,1,0:T(8,128)(2,1)} reshape(bf16[4,4096]{1,0:T(4,128)(2,1)} %param.14) | data formatting | bytes 65536 | tf_op jit(solution)/shard_map/reshape | solution.py:539
  9.3 1.5 %copy.17 = bf16[8,4,8,64]{3,2,1,0:T(8,128)(2,1)} copy(bf16[8,4,8,64]{3,0,2,1:T(8,128)(2,1)} %bitcast.21) | data formatting | bytes 65536 | tf_op jit(solution)/shard_map/transpose | solution.py:539
  10.8 1.6 %reshape.41 = bf16[8,4,512]{2,1,0:T(4,128)(2,1)} reshape(bf16[8,4,8,64]{3,2,1,0:T(8,128)(2,1)} %copy.17) | data formatting | bytes 65536 | tf_op jit(solution)/shard_map/reshape | solution.py:539
  12.3 1.4 %bitcast_convert_fusion.scales_ref = f32[64,512]{1,0:T(8,128)} fusion(bf16[8,4,512]{2,1,0:T(4,128)(2,1)} %reshape.41), kind=kLoop, calls=%fused_computation | loop fusion | flops 32768 | bytes 163840 | tf_op jit(solution)/shard_map/reshape | solution.py:540
  13.8 0.0 slice-done
  13.8 0.7 fusion.1.allow_ref
  14.5 0.0 copy-done.9
  14.5 0.1 reshape.51
  14.6 0.7 pad.15.vw_ref
  15.3 0.0 copy-done
  15.3 0.0 copy-done.1
  15.3 0.0 copy-done.8
  15.3 0.0 copy-start.2
  15.3 0.9 copy-done.2
  16.2 0.0 copy-start.3
  16.2 0.9 copy-done.3
  17.2 0.0 copy-start.4
  17.2 0.9 copy-done.4
  18.1 0.0 copy-start.5
  18.1 0.8 copy-done.5
  18.8 0.0 copy-start.6
  18.9 0.9 copy-done.6
  19.8 93.0 %distill.1 = (f32[1,1]{1,0:T(1,128)}, f32[32,256]{1,0:T(8,128)S(1)}) custom-call(bf16[4,2,32,512]{3,2,1,0:T(8,128)(2,1)S(1)} %bitcast.16, s32[512,1024]{1,0:T(8,128)S(1)} %copy-done, f32[64,512]{1,0:T(8,128)S(1)} %copy-done.2, bf16[4,2,32,512]{3,2,1,0:T(8,128)(2,1)S(1)} %reshape.44.resid_ref, f32[8,512]{1,0:T(8,128)S(1)} %broadcast_in_dim.16.gain_ref, ...), custom_call_target="tpu_custom_call" | custom-call | tf_op jit(solution)/shard_map/distill/pallas_call | solution.py:551
  112.7 0.0 copy-start.7
  112.7 0.6 copy-done.7
  114.0 1.4 %copy.24 = f32[28,256]{1,0:T(8,128)} copy(f32[28,256]{1,0:T(8,128)} %bitcast.18) | data formatting | bytes 57344
  (1 shorter events, 0.0 us)
Async XLA Ops:
  2.0 11.8 %slice-start = ((s32[256]{0:T(256)}), s32[64]{0:T(128)S(1)}, s32[]{:S(2)}) async-start(s32[256]{0:T(256)} %param.22), calls=%async_computation | async-start | bytes 1024 | tf_op jit(solution)/shard_map/slice | solution.py:543
  2.0 12.5 %copy-start.9 = (bf16[8,64]{1,0:T(8,128)(2,1)S(1)}, bf16[8,64]{1,0:T(8,128)(2,1)}, u32[]{:S(2)}) copy-start(bf16[8,64]{1,0:T(8,128)(2,1)} %param.16) | copy-start | bytes 3076
  2.0 13.3 %copy-start = (s32[512,1024]{1,0:T(8,128)S(1)}, s32[512,1024]{1,0:T(8,128)}, u32[]{:S(2)}) copy-start(s32[512,1024]{1,0:T(8,128)} %codes_ref.1) | copy-start | bytes 6291460
  2.0 13.2 %copy-start.1 = (bf16[256,1792]{1,0:T(8,128)(2,1)S(1)}, bf16[256,1792]{1,0:T(8,128)(2,1)}, u32[]{:S(2)}) copy-start(bf16[256,1792]{1,0:T(8,128)(2,1)} %q_ref.1) | copy-start | bytes 2752516
  2.0 13.2 %copy-start.8 = (s32[2048,1]{0,1:T(1,128)S(1)}, s32[2048,1]{0,1:T(1,128)}, u32[]{:S(2)}) copy-start(s32[2048,1]{0,1:T(1,128)} %param.18) | copy-start | bytes 24580
  15.3 0.9 copy-start.2
  16.2 0.9 copy-start.3
  17.2 0.9 copy-start.4
  18.1 0.8 copy-start.5
  18.8 0.9 copy-start.6
  112.7 0.6 copy-start.7

commit v2 on v0

v2 whole, which is shorter than its diff:
```python
import functools
from types import SimpleNamespace

import jax
import jax.numpy as jnp
from jax import lax
from jax.experimental import pallas as pl
from jax.experimental.pallas import tpu as pltpu
from jax.sharding import PartitionSpec as P

HT = 4096
GROUP = 128
HEAD = 128
EPS = 1e-06
F32, BF16 = jnp.float32, jnp.bfloat16
MESH = pl.DeviceIdType.MESH

N = 8
ZH = 4
LEAD = 64
QW = 1792
KVW = 256
CHUNKS = (1024, 768)
WIDTHS = (1024 + 128, 768)
LOSS_ROW = 28


def ring_buffers(name, rows, width):
    block, sems = pltpu.VMEM((2, rows, width), BF16), pltpu.SemaphoreType.DMA((6,))
    spec = {f"{name}_{part}": block for part in ("relay", "near", "added", "summed")}
    return spec | {f"{name}_s": sems, f"{name}_r": sems}


def scratch_spec():
    dma, vmem = pltpu.SemaphoreType.DMA, pltpu.VMEM
    return dict(
        codes=vmem((512, 1024), jnp.int32),
        routes=pltpu.SMEM((2048,), jnp.int32),
        x=vmem((4, 2, 32, 512), BF16),
        xb=vmem((2, 4, 32, 512), BF16),
        stu=vmem((LEAD, QW), BF16),
        stus=vmem((8, LEAD, KVW), BF16),
        residt=vmem((512, 256), BF16),
        resid=vmem((4, 2, 32, 512), BF16),
        resb=vmem((2, 4, 32, 512), BF16),
        gainb=vmem((2, 8, 512), F32),
        vwp=vmem((32, KVW), BF16),
        vw=vmem((8, 32, KVW), BF16),
        perm=vmem((8, 256, 128), jnp.int32),
        scp=vmem((64, 512), F32),
        spread=vmem((512, 512), BF16),
        wbuf=vmem((512, 1024), BF16),
        part=vmem((ZH, 128, 1024), BF16),
        half_out=vmem((ZH, 128, 1024), BF16),
        half_in=vmem((ZH, 128, 1024), BF16),
        proj=vmem((2, 2, 4, 64, QW), BF16),
        q=vmem((LEAD, QW), BF16),
        k=vmem((LEAD, KVW), BF16),
        sb=vmem((8, LEAD, KVW), BF16),
        pvs=vmem((8, LEAD, KVW), BF16),
        pvr=vmem((8, LEAD, KVW), BF16),
        probs=vmem((2, 7 * LEAD, LEAD), BF16),
        g1=vmem((8, LEAD, KVW), BF16),
        lost=vmem((8, 8, 128), F32),
        g2s=vmem((8, 32, KVW), BF16),
        g2r=vmem((8, 32, KVW), BF16),
        g3=vmem((8, 32, KVW), BF16),
        **ring_buffers("t1", 64, 1024),
        **{f"pbuf{i}": vmem((ZH, 32, width), BF16) for i, width in enumerate(WIDTHS)},
        **ring_buffers("t4a", 16, WIDTHS[0]),
        **ring_buffers("t4b", 16, WIDTHS[1]),
        **{f"osend{i}": vmem((8, 16, width // 2), BF16) for i, width in enumerate(CHUNKS)},
        **{f"trecv{i}": vmem((8, 16, width // 2), BF16) for i, width in enumerate(CHUNKS)},
        in_sem=dma((8,)),
        sib_s=dma((6,)),
        sib_r=dma((6,)),
        p_s=dma((9,)),
        p_r=dma((8, 2)),
        psib_s=dma((8,)),
        psib_r=dma((8,)),
        **{
            name + end: dma((8,))
            for name in ("py", "stu", "vwz", "vwy", "pv", "t5a", "t5b", "g1", "loss", "g2", "g3")
            for end in ("_s", "_r")
        },
    )


def dot(a, b, dims=((1,), (0,))):
    return lax.dot_general(a, b, (dims, ((), ())), preferred_element_type=F32)


def remote(src, dst, send, recv, **device):
    return pltpu.make_async_remote_copy(
        src_ref=src,
        dst_ref=dst,
        send_sem=send,
        recv_sem=recv,
        device_id=device,
        device_id_type=MESH,
    )


class Flow:
    def __init__(self):
        self.sent, self.due = [], []

    def start(self, *copies, due=()):
        for copy in copies:
            copy.start()
        self.sent += copies
        self.due += list(due)

    def wait(self, *copies):
        for copy in copies:
            copy.wait_recv()
            self.due = [left for left in self.due if left is not copy]

    def finish(self):
        for copy in list(self.due):
            self.wait(copy)
        for copy in self.sent:
            copy.wait_send()


class Exchange:
    def __init__(self, axis, me, src, dst, send, recv):
        self.axis, self.me, self.src, self.dst = axis, me, src, dst
        self.send, self.recv = send, recv

    def each(self, act):
        def body(step, carry):
            act(lax.rem(self.me + step, N))
            return carry

        lax.fori_loop(1, N, body, 0)

    def copy(self, peer, slot):
        return remote(
            self.src(peer),
            self.dst(slot),
            self.send.at[peer],
            self.recv.at[slot],
            **{self.axis: peer},
        )

    def start(self):
        self.each(lambda peer: self.copy(peer, self.me).start())

    def wait_recv(self):
        self.each(lambda peer: self.copy(peer, peer).wait_recv())

    def wait_send(self):
        self.each(lambda peer: self.copy(peer, self.me).wait_send())


def split_sum(total):
    high = total.astype(BF16).astype(F32)
    lane = lax.broadcasted_iota(jnp.int32, (total.shape[0], 128), 1)
    return jnp.where(lane == 0, high, jnp.where(lane == 1, total - high, 0.0)).astype(BF16)


def loss_row(value):
    row, lane = iotas(32, KVW)
    spread = jnp.full((32, KVW), value, F32)
    high = spread.astype(BF16).astype(F32)
    middle = (spread - high).astype(BF16).astype(F32)
    low = spread - high - middle
    picked = jnp.where(lane == 0, high, jnp.where(lane == 1, middle, jnp.where(lane == 2, low, 0.0)))
    return jnp.where(row == LOSS_ROW, picked, 0.0)


def loss_of(block):
    row, _ = iotas(32, KVW)
    return jnp.sum(jnp.where(row == LOSS_ROW, block, 0.0))


def ring_sum(out, at, mine, other, width):
    mine, other = mine.astype(F32), other.astype(F32)
    total = mine + other
    out[at, :, :width] = total[:, :width].astype(BF16)
    if out.shape[2] > width:
        out[at, :, width:] = split_sum(jnp.sum(total[:, width:], axis=1, keepdims=True))


def transpose_runs(a):
    lane = lax.broadcasted_iota(jnp.int32, a[0].shape, 1)
    for step in (4, 2, 1):
        upper = (lane & (16 * step)) != 0
        new = list(a)
        for j in range(8):
            if j & step == 0:
                low, high = a[j], a[j + step]
                new[j] = jnp.where(upper, pltpu.roll(high, 16 * step, 1), low)
                new[j + step] = jnp.where(upper, high, pltpu.roll(low, 128 - 16 * step, 1))
        a = new
    return a


def one_hot(hit):
    return jnp.where(hit, 1.0, 0.0).astype(BF16)


def iotas(*shape):
    return [lax.broadcasted_iota(jnp.int32, shape, axis) for axis in range(2)]


def kernel(
    total_count,
    names,
    x_ref,
    codes_ref,
    scales_ref,
    residt_ref,
    gain_ref,
    proj_ref,
    routes_ref,
    stu_ref,
    seg_ref,
    vw_ref,
    q_ref,
    k_ref,
    loss_ref,
    grad_ref,
    *scratch,
):
    m = SimpleNamespace(**dict(zip(names, scratch)))
    flow = Flow()

    d, f, t = lax.axis_index("dp"), lax.axis_index("fsdp"), lax.axis_index("tensor")
    zh, c = lax.div(t, 2), lax.rem(t, 2)
    other = 1 - c
    sib = t + 1 - 2 * c
    zp, zm = lax.rem(t + 2, N), lax.rem(t + 6, N)
    fz = f + 1 - 2 * lax.rem(f, 2)
    xp, xm = lax.rem(f + 2, N), lax.rem(f + 6, N)
    xpz, xmz = xp + 1 - 2 * lax.rem(xp, 2), xm + 1 - 2 * lax.rem(xm, 2)
    xf = lax.rem(f + 4, N)
    xfz = xf + 1 - 2 * lax.rem(xf, 2)

    barrier = pltpu.get_barrier_semaphore()

    def greet(step, carry):
        for axis, me in (("tensor", t), ("fsdp", f), ("dp", d)):
            pl.semaphore_signal(
                barrier, inc=1, device_id={axis: lax.rem(me + step, N)}, device_id_type=MESH
            )
        return carry

    lax.fori_loop(1, N, greet, 0)

    zl, xi = lax.rem(f, 2), lax.div(f, 2)
    inputs = [
        (codes_ref, m.codes),
        (x_ref, m.x),
        (stu_ref.at[pl.ds(0, LEAD)], m.stu),
        (proj_ref, m.proj.at[c, zl, xi]),
        (residt_ref, m.residt),
        (q_ref.at[pl.ds(0, LEAD)], m.q),
        (k_ref.at[pl.ds(0, LEAD)], m.k),
        (routes_ref, m.routes),
    ]
    inputs = [pltpu.make_async_copy(src, dst, m.in_sem.at[i]) for i, (src, dst) in enumerate(inputs)]
    codes_in, x_in, stu_in, proj_in, resid_in, q_in, k_in, routes_in = inputs
    for copy in inputs:
        copy.start()

    row, col = iotas(512, 512)
    own_order = ((row >> 4) & 7) * 64 + (row & 15) * 4 + (row >> 7)
    m.spread[...] = one_hot(own_order == col)

    scales = jnp.concatenate([scales_ref[...].astype(F32), jnp.zeros((4, HT), F32)], axis=0)
    scales = jnp.concatenate([scales[:, j * 512 : (j + 1) * 512] for j in range(8)], axis=0)
    scales = dot(scales.astype(BF16), m.spread[...], ((1,), (1,)))
    for level in range(4):
        lanes = slice(level * 128, (level + 1) * 128)
        for j, piece in enumerate(transpose_runs([scales[8 * j : 8 * j + 8, lanes] for j in range(8)])):
            m.scp[8 * j : 8 * j + 8, lanes] = piece

    def shuffle(i, carry):
        at = pl.ds(pl.multiple_of(i * 32, 32), 32)
        far_at = pl.ds(pl.multiple_of(i * 32 + 256, 32), 32)
        words = []
        for j in range(8):
            lanes = slice(j * 128, (j + 1) * 128)
            words.append(m.codes[at, lanes] | (m.codes[far_at, lanes] << 16))
        for j, piece in enumerate(transpose_runs(words)):
            m.perm[j, at, :] = piece
        return carry

    def slots(ref):
        return lambda slot: ref.at[slot]

    def block(owner):
        return m.proj.at[c, lax.rem(owner, 2), lax.div(owner, 2)]

    def half_block(owner, half):
        return m.proj.at[c, lax.rem(owner, 2), lax.div(owner, 2), pl.ds(32 * half, 32)]

    def piece_at(place):
        down, along = lax.div(place, 2), lax.rem(place, 2)
        return pl.ds(pl.multiple_of(down * 16, 16), 16), pl.ds(pl.multiple_of(along * 896, 128), 896)

    def piece(owner, place):
        return m.proj.at[(c, lax.rem(owner, 2), lax.div(owner, 2)) + piece_at(place)]

    def pass_on(i, owner, half=None, src=None, **device):
        dst = block(owner) if half is None else half_block(owner, half)
        return remote(dst if src is None else src, dst, m.p_s.at[i], m.p_r.at[owner, half or 0], **device)

    to_z = remote(proj_ref.at[piece_at(d)], piece(f, d), m.p_s.at[0], m.p_r.at[f, 0], fsdp=fz)
    from_z = remote(proj_ref.at[piece_at(d)], piece(fz, d), m.p_s.at[0], m.p_r.at[fz, 0], fsdp=fz)
    pieces = Exchange("dp", d, lambda peer: piece(fz, d), lambda slot: piece(fz, slot), m.py_s, m.py_r)
    near_same = [pass_on(1, owner, fsdp=fz) for owner in (xm, xp)]
    near_other = [pass_on(1, owner, fsdp=fz) for owner in (xmz, xpz)]
    far_same = [pass_on(1, xf, half, fsdp=fz) for half in range(2)]
    far_other = [pass_on(1, xfz, half, fsdp=fz) for half in range(2)]
    def block_to_sibling(owner, slot):
        dst = m.proj.at[slot, lax.rem(owner, 2), lax.div(owner, 2)]
        return remote(block(owner), dst, m.psib_s.at[owner], m.psib_r.at[owner], tensor=sib)

    owners = (f, xm, xp, xf, fz, xmz, xpz, xfz)
    proj_here = [block_to_sibling(owner, other) for owner in owners]

    def share(*places):
        flow.start(*(block_to_sibling(owners[i], c) for i in places), due=[proj_here[i] for i in places])

    value_rows = Exchange("tensor", t, lambda peer: m.vwp, slots(m.vw), m.vwz_s, m.vwz_r)
    value_slices = Exchange("dp", d, lambda peer: m.vw.at[d], slots(m.vw), m.vwy_s, m.vwy_r)

    class ValueRows:
        def start(self):
            @pl.when(t == d)
            def _():
                m.vw[d] = m.vwp[...]
                value_rows.start()

        def wait_recv(self):
            @pl.when(t != d)
            def _():
                value_rows.copy(d, d).wait_recv()

        def wait_send(self):
            @pl.when(t == d)
            def _():
                value_rows.wait_send()

    sent_rows = ValueRows()
    row, col = iotas(32, 28)
    m.vwp[...] = dot(one_hot(row == col), vw_ref[...]).astype(BF16)

    pl.semaphore_wait(barrier, 3 * (N - 1))
    flow.start(to_z, due=[from_z])
    flow.start(pass_on(1, f, src=proj_ref, fsdp=xp), pass_on(2, f, src=proj_ref, fsdp=xm), due=near_same)
    flow.start(sent_rows, due=[sent_rows])

    codes_in.wait()
    lax.fori_loop(0, 8, shuffle, 0, unroll=4)
    x_in.wait()
    for b in range(4):
        m.xb[0, b] = m.x[b, c]
        m.xb[1, b] = m.x[b, other]

    def partial(r):
        z = lax.rem(zh + r, ZH)

        def dequantize(s, carry):
            slice_at = 2 * z + s
            sc = m.scp[pl.ds(pl.multiple_of(slice_at * 8, 8), 8), :]
            for g in range(4):
                at = slice(g * GROUP, (g + 1) * GROUP)
                words = m.perm[slice_at, g % 2 * GROUP : (g % 2 + 1) * GROUP, :]
                for level in range(4):
                    value = lax.shift_right_logical(words, g // 2 * 16 + 4 * level) & 15
                    value = value.astype(F32) - 8.0
                    value = value * sc[g : g + 1, level * 128 : (level + 1) * 128]
                    lanes = pl.ds(pl.multiple_of(s * 512 + level * 128, 128), 128)
                    m.wbuf[at, lanes] = value.astype(BF16)
            return carry

        lax.fori_loop(0, 2, dequantize, 0)
        rows = m.xb[...].reshape(256, 512)
        for s in range(2):
            lanes = slice(s * 512, (s + 1) * 512)
            acc = dot(rows, m.wbuf[:, lanes]).astype(BF16)
            acc = dot(acc, m.spread[...]).astype(BF16)
            m.part[r, :, lanes] = acc[0:128]
            m.half_out[r, :, lanes] = acc[128:256]

    def to_sibling(i, src, dst):
        return remote(src, dst, m.sib_s.at[i], m.sib_r.at[i], tensor=sib)

    halves = [to_sibling(r, m.half_out.at[r], m.half_in.at[r]) for r in range(ZH)]
    resid_there = to_sibling(4, m.resid.at[:, other], m.resb.at[c])
    resid_here = to_sibling(4, m.resid.at[:, other], m.resb.at[other])
    gain_there = to_sibling(5, m.gainb.at[c], m.gainb.at[c])
    gain_here = to_sibling(5, m.gainb.at[c], m.gainb.at[other])

    def add_half(r):
        flow.wait(halves[r])
        m.part[r] = (m.part[r].astype(F32) + m.half_in[r].astype(F32)).astype(BF16)

    students = Exchange("fsdp", f, slots(m.stus), slots(m.sb), m.stu_s, m.stu_r)
    value_parts = Exchange("fsdp", f, slots(m.pvs), slots(m.pvr), m.pv_s, m.pv_r)
    targets = [
        Exchange("dp", d, slots(m.osend0), slots(m.trecv0), m.t5a_s, m.t5a_r),
        Exchange("dp", d, slots(m.osend1), slots(m.trecv1), m.t5b_s, m.t5b_r),
    ]
    grads1 = Exchange("fsdp", f, lambda peer: m.g1.at[f], slots(m.g1), m.g1_s, m.g1_r)
    losses = Exchange("fsdp", f, lambda peer: m.lost.at[f], slots(m.lost), m.loss_s, m.loss_r)
    grads2 = Exchange("tensor", t, slots(m.g2s), slots(m.g2r), m.g2_s, m.g2_r)
    grads3 = Exchange("dp", d, lambda peer: m.g3.at[d], slots(m.g3), m.g3_s, m.g3_r)

    def ring(src, name, half):
        relay, near, added, summed, send, recv = (
            getattr(m, f"{name}_{end}") for end in ("relay", "near", "added", "summed", "s", "r")
        )
        low, high = pl.ds(0, half), pl.ds(half, half)
        far = [
            remote(src(2, low), relay.at[0], send.at[0], recv.at[0], tensor=zp),
            remote(src(2, high), relay.at[1], send.at[1], recv.at[1], tensor=zm),
        ]
        direct = [
            remote(src(1, high), near.at[0], send.at[2], recv.at[2], tensor=zp),
            remote(src(3, low), near.at[1], send.at[3], recv.at[3], tensor=zm),
        ]
        sums = [
            remote(added.at[0], summed.at[0], send.at[4], recv.at[4], tensor=zp),
            remote(added.at[1], summed.at[1], send.at[5], recv.at[5], tensor=zm),
        ]
        return far, direct, sums

    far, direct, sums = ring(lambda r, rows: m.part.at[r, rows], "t1", 64)
    partial(2)
    flow.start(halves[2], due=[halves[2]])
    partial(1)
    flow.start(halves[1], due=[halves[1]])
    add_half(2)
    flow.start(*far, due=far)
    partial(3)
    flow.start(halves[3], due=[halves[3]])
    add_half(1)
    flow.start(direct[0], due=direct[:1])
    proj_in.wait()
    share(0)
    flow.wait(from_z, sent_rows)
    flow.start(pieces, due=[pieces])
    partial(0)
    flow.start(halves[0], due=[halves[0]])
    add_half(3)
    flow.start(direct[1], due=direct[1:])
    flow.start(value_slices, due=[value_slices])

    resid_in.wait()
    row, col = iotas(512, 512)
    m.resid[...] = dot(m.residt[...], one_hot(row == col), ((0,), (0,))).astype(BF16).reshape(4, 2, 32, 512)
    for b in range(4):
        m.resb[c, b] = m.resid[b, c]
    row, col = iotas(64, 512)
    gain = dot(gain_ref[...], one_hot((col & 63) == row))
    row, col = iotas(8, 512)
    gain = jnp.sum(jnp.where((col >> 6) == row, gain, 0.0), axis=0, keepdims=True)
    m.gainb[c] = jnp.broadcast_to(gain, (8, 512))
    flow.start(resid_there, gain_there, due=[resid_here, gain_here])
    add_half(0)

    flow.wait(*near_same)
    flow.start(pass_on(3, xm, 0, fsdp=xp), pass_on(4, xp, 1, fsdp=xm), due=far_same)
    share(1, 2)
    flow.wait(pieces)
    flow.start(pass_on(5, fz, fsdp=xp), pass_on(6, fz, fsdp=xm), due=near_other)
    share(4)
    flow.wait(far[0])
    ring_sum(m.t1_added, 0, m.part[1, 0:64], m.t1_relay[0], 1024)
    flow.start(sums[0], due=sums[:1])
    flow.wait(far[1])
    ring_sum(m.t1_added, 1, m.part[3, 64:128], m.t1_relay[1], 1024)
    flow.start(sums[1], due=sums[1:])

    stu_in.wait()
    row, col = iotas(896, 1024)
    pad = one_hot(((col >> 5) * 28 + (col & 31) == row) & ((col & 31) < 28))
    for j in range(2):
        padded = dot(m.stu[:, j * 896 : (j + 1) * 896], pad).astype(BF16)
        for i in range(4):
            m.stus[4 * j + i] = padded[:, i * KVW : (i + 1) * KVW]
    m.sb[f] = m.stus[f]

    places = jnp.broadcast_to(seg_ref[0:1, 0:128].astype(F32), (128, 128))
    same = places == jnp.transpose(places)
    row, col = iotas(128, 128)
    allow = jnp.where(same & (row >= col), 1.0, 0.0)[:LEAD, :LEAD]
    allow = jnp.concatenate([allow] * 7, axis=0)
    q_in.wait()
    k_in.wait()
    for g in range(2):
        heads = [m.q[:, (g * 7 + h) * HEAD : (g * 7 + h + 1) * HEAD] for h in range(7)]
        scores = dot(jnp.concatenate(heads, axis=0), m.k[:, g * HEAD : (g + 1) * HEAD], ((1,), (1,)))
        scores = jnp.where(allow > 0.0, scores * HEAD ** (-0.5), -1e30)
        weights = jnp.exp(scores - jnp.max(scores, axis=1, keepdims=True))
        m.probs[g] = (weights / jnp.sum(weights, axis=1, keepdims=True)).astype(BF16)

    routes_in.wait()
    row, col = iotas(64, 32)
    place = ((d * N + f) * N + t) * 4
    wanted = jnp.full((64, 32), -1, jnp.int32)
    for j in range(4):
        wanted = jnp.where((col >> 3) == j, m.routes[place + j], wanted)
    select = one_hot(((row >> 3) == wanted) & ((row & 7) == (col & 7)))
    lead = lax.broadcasted_iota(jnp.int32, (LEAD, HEAD), 0) >> 3
    mask = jnp.zeros((LEAD, HEAD), F32)
    for source in range(N):
        for j in range(4):
            hit = m.routes[((source * N + f) * N + t) * 4 + j] == d
            mask = jnp.where(lead == source, jnp.maximum(mask, jnp.where(hit, 1.0, 0.0)), mask)

    flow.wait(*far_same)
    share(3)
    flow.wait(*near_other)
    flow.start(pass_on(7, xmz, 0, fsdp=xp), pass_on(8, xpz, 1, fsdp=xm), due=far_other)
    share(5, 6)
    flow.wait(*direct, *sums, resid_here, gain_here)
    flow.start(students, due=[students])

    lower = m.part[0, 0:64].astype(F32) + m.t1_summed[0].astype(F32) + m.t1_near[1].astype(F32)
    upper = m.part[0, 64:128].astype(F32) + m.t1_near[0].astype(F32) + m.t1_summed[1].astype(F32)
    out = jnp.concatenate([lower, upper], axis=0)
    power = jnp.zeros((128, 1), F32)
    scaled = []
    for s in range(2):
        hidden = out[:, s * 512 : (s + 1) * 512] + m.resb[s].reshape(128, 512).astype(F32)
        power = power + jnp.sum(hidden * hidden, axis=1, keepdims=True)
        scaled.append((hidden * m.gainb[s, 0:1, :]).astype(BF16))
    m.pbuf0[:, :, CHUNKS[0] :] = split_sum(power).reshape(ZH, 32, 128)
    flow.wait(*far_other)
    share(7)
    flow.wait(*proj_here)

    def ahead(pbuf):
        return lambda r, rows: pbuf.at[lax.rem(zh + r, ZH), rows]

    rings = [ring(ahead(m.pbuf0), "t4a", 16), ring(ahead(m.pbuf1), "t4b", 16)]
    pbufs = (m.pbuf0, m.pbuf1)
    for i in range(2):
        for j in range(CHUNKS[i] // 256):
            lanes = slice(j * 256, (j + 1) * 256)
            from_lanes = slice(i * CHUNKS[0] + j * 256, i * CHUNKS[0] + (j + 1) * 256)
            acc = jnp.zeros((128, 256), F32)
            for s in range(2):
                rows = [m.proj[s, owner % 2, owner // 2, :, from_lanes] for owner in range(8)]
                acc = acc + dot(scaled[s], jnp.concatenate(rows, axis=0))
            pbufs[i][:, :, lanes] = acc.astype(BF16).reshape(ZH, 32, 256)
        flow.start(*rings[i][0], *rings[i][1], due=rings[i][0] + rings[i][1])
    for i, name in enumerate(("t4a", "t4b")):
        far4, direct4, sums4 = rings[i]
        relay, added = getattr(m, f"{name}_relay"), getattr(m, f"{name}_added")
        for way, r in enumerate((1, 3)):
            flow.wait(far4[way])
            mine = pbufs[i][lax.rem(zh + r, ZH), 16 * way : 16 * way + 16]
            ring_sum(added, way, mine, relay[way], CHUNKS[i])
            flow.start(sums4[way], due=[sums4[way]])

    flow.wait(students, value_slices)
    rows_of_value = m.vw[...].reshape(8 * 32, KVW)
    value_part = dot(m.sb[...].reshape(8 * LEAD, KVW), rows_of_value)
    m.pvs[...] = value_part.reshape(8, LEAD, KVW).astype(BF16)
    m.pvr[f] = m.pvs[f]

    row_scale = None
    for i, name in enumerate(("t4a", "t4b")):
        _, direct4, sums4 = rings[i]
        flow.wait(*direct4, *sums4)
        near, summed = getattr(m, f"{name}_near"), getattr(m, f"{name}_summed")
        own = pbufs[i][zh].astype(F32)
        lower = own[0:16] + summed[0].astype(F32) + near[1].astype(F32)
        upper = own[16:32] + near[0].astype(F32) + summed[1].astype(F32)
        total = jnp.concatenate([lower, upper], axis=0)
        if i == 0:
            power = jnp.sum(total[:, CHUNKS[0] :], axis=1, keepdims=True)
            row_scale = lax.rsqrt(power / HT + EPS)
        routed = dot(select, (total[:, : CHUNKS[i]] * row_scale).astype(BF16))
        half = CHUNKS[i] // 2
        osend, trecv = getattr(m, f"osend{i}"), getattr(m, f"trecv{i}")
        osend[...] = jnp.concatenate(
            [routed[:, :half].reshape(8, 8, half), routed[:, half:].reshape(8, 8, half)], axis=1
        ).astype(BF16)
        trecv[d] = osend[d]
        flow.start(targets[i], due=[targets[i]])
    flow.start(value_parts, due=[value_parts])
    flow.wait(value_parts)
    values = m.pvr[0].astype(F32)
    for j in range(1, 8):
        values = values + m.pvr[j].astype(F32)
    values = values.astype(BF16)
    attended = [dot(m.probs[g], values[:, g * HEAD : (g + 1) * HEAD]) for g in range(2)]

    lost = jnp.zeros((LEAD, HEAD), F32)
    pieces_of = ([], [])
    for i in range(2):
        flow.wait(targets[i])
        received = getattr(m, f"trecv{i}")[...].astype(F32)
        per_half = CHUNKS[i] // 2 // HEAD
        for j in range(2 * per_half):
            at, lane = j // per_half * 8, j % per_half * HEAD
            wanted = received[:, at : at + 8, lane : lane + HEAD].reshape(LEAD, HEAD)
            head = i * (CHUNKS[0] // HEAD) + j
            g, h = head // 7, head % 7
            diff = attended[g][h * LEAD : (h + 1) * LEAD] - wanted
            masked = diff * mask
            lost = lost + masked * diff
            pieces_of[g].append((2.0 * masked / QW).astype(BF16))
    for g in range(2):
        grad = dot(m.probs[g], jnp.concatenate(pieces_of[g], axis=0), ((0,), (0,)))
        m.g1[f, :, g * HEAD : (g + 1) * HEAD] = grad.astype(BF16)
    flow.start(grads1, due=[grads1])
    lost = lost.reshape(8, 8, 128).sum(axis=0)
    m.lost[f] = lost
    flow.start(losses, due=[losses])
    flow.wait(grads1)
    grad = dot(m.sb[...].reshape(8 * LEAD, KVW), m.g1[...].reshape(8 * LEAD, KVW), ((0,), (0,)))
    flow.wait(losses)
    tail = loss_row(jnp.sum(m.lost[...]))
    for j in range(N):
        m.g2s[j] = (grad[32 * j : 32 * j + 32] + tail).astype(BF16)
    m.g2r[t] = m.g2s[t]
    flow.start(grads2, due=[grads2])
    flow.wait(grads2)
    row, _ = iotas(32, KVW)
    total = jnp.sum(m.g2r[...].astype(F32), axis=0)
    m.g3[d] = jnp.where(row < LOSS_ROW, total, loss_row(loss_of(total))).astype(BF16)
    flow.start(grads3, due=[grads3])
    flow.wait(grads3)
    total = jnp.sum(m.g3[...].astype(F32), axis=0)
    grad_ref[...] = total[0:LOSS_ROW]
    loss_ref[0, 0] = loss_of(total) / total_count
    flow.finish()


def local(
    teacher_in,
    codes,
    scales,
    teacher_resid,
    teacher_gain,
    projector,
    routes,
    student_in,
    queries,
    keys,
    segments,
    value_weight,
):
    spec = scratch_spec()
    vmem = pl.BlockSpec(memory_space=pltpu.VMEM)
    smem = pl.BlockSpec(memory_space=pltpu.SMEM)
    hbm = pl.BlockSpec(memory_space=pltpu.HBM)
    loss, grad = pl.pallas_call(
        functools.partial(kernel, float(16384 * QW), tuple(spec)),
        out_shape=(
            jax.ShapeDtypeStruct((1, 1), F32),
            jax.ShapeDtypeStruct((28, KVW), F32),
        ),
        in_specs=[hbm, hbm, vmem, hbm, vmem, hbm, hbm, hbm, vmem, vmem, hbm, hbm],
        out_specs=(smem, vmem),
        scratch_shapes=list(spec.values()),
        compiler_params=pltpu.CompilerParams(
            collective_id=0, has_side_effects=True, vmem_limit_bytes=56 * 1024 * 1024
        ),
        name="distill",
    )(
        teacher_in.reshape(4, 2, 32, 512),
        codes,
        scales,
        teacher_resid.transpose(1, 2, 0).reshape(512, 256),
        teacher_gain,
        projector.reshape(64, QW),
        routes.reshape(2048),
        student_in,
        segments.reshape(1, 256),
        value_weight,
        queries,
        keys,
    )
    return loss[0, 0], grad


def solution(mesh):
    return jax.shard_map(
        local,
        mesh=mesh,
        in_specs=(
            P(("dp", "fsdp"), "tensor"),
            P("tensor", None),
            P("tensor", None),
            P(("dp", "fsdp"), None, "tensor"),
            P(None, "tensor"),
            P("fsdp", "tensor", None),
            P(),
            P(("dp", "fsdp", "tensor"), None),
            P(("dp", "fsdp", "tensor"), None),
            P(("dp", "fsdp", "tensor"), None),
            P(("dp", "fsdp", "tensor")),
            P(("fsdp", "tensor"), None),
        ),
        out_specs=(P(), P(("fsdp", "tensor"), None)),
        check_vma=False,
    )
```

time: 547 us -> 89 us (0.16); the launches traced: 538 us -> 88.7 us
  blocking collectives: 225 us -> 0 us
  waiting for transfers between devices: 213 us -> 0 us
  Pallas kernels: 0 us -> 84.9 us
  local copies, waits for them, and re-layouts: 43.4 us -> 1.38 us
  matrix products: 17.1 us -> 0 us
  between operations: 17.8 us -> 2.4 us
  other arithmetic: 15 us -> 0 us
  starting transfers between devices: 6.5 us -> 0 us
    psum x3 -> x0, blocking collectives: 139 us -> none  [the longest x1 101 us: local(): lax.psum(loss_term, ('dp', 'fsdp', 'tensor')) / (total_rows * query_width)]
    psum x2 -> x0, waiting for transfers between devices: 116 us -> none  [the longest x1 72.6 us: local(): target = lax.psum(target_part.astype(jnp.bfloat16), 'tensor')]
    unnamed x5 -> x0, waiting for transfers between devices: 94.1 us -> none
    all_gather x1 -> x0, blocking collectives: 85.9 us -> none  [local(): lax.all_gather(value_weight, ('fsdp', 'tensor'), axis=0, tiled=True)]
    pallas_call x0 -> x1, Pallas kernels: none -> 84.9 us  [local(): pl.pallas_call(functools.partial(kernel, float(16384 * QW), tuple(spec)),...]
    sub x2 -> x0, local copies, waits for them, and re-layouts: 20.2 us -> none  [dequantize(): levels = unpack_levels(codes).astype(jnp.float32) - 8.0]
    dot_general x7 -> x0, matrix products: 13.2 us -> none  [the longest x1 3.39 us: local(): jnp.einsum('rkc,kcq->rq', picked, lax.all_gather(projector, 'fsdp', axis=...]
    broadcast_in_dim x2 -> x0, local copies, waits for them, and re-layouts: 9.56 us -> none  [the longest x1 9.49 us: dequantize(): spread = jnp.repeat(scales.astype(jnp.float32), GROUP, axis=0)]
  transfers between devices with their start and end apart: 5 -> 0, of which waited for: 4 -> 0; matrix products, arithmetic and copies ran while one was open for 4% -> 0% of each run, Pallas kernels for 0% -> 0%
where the time goes in v2:
time: 89 us; the launch traced here: 88.7 us
  Pallas kernels  84.9 us (95%)
  between operations  2.4 us (3%)
  local copies, waits for them, and re-layouts  1.38 us (2%)
    pallas_call x1, Pallas kernels, local(): pl.pallas_call(functools.partial(kernel, float(16384 * QW), tuple(spec)),...  84.9 us

profile of v2, /device:TPU:1, one launch (start us, length us, event | category | flops | bytes accessed | tf_op | source)
XLA Modules:
  0.0 88.7 jit_solution(13030439736973767188)
XLA Ops:
  0.6 84.9 %distill.1 = (f32[1,1]{1,0:T(1,128)}, f32[28,256]{1,0:T(8,128)}) custom-call(bf16[4,2,32,512]{3,2,1,0:T(8,128)(2,1)} %bitcast.8, s32[512,1024]{1,0:T(8,128)} %codes_ref.1, bf16[4,4096]{1,0:T(4,128)(2,1)} %scales_ref.1, bf16[512,256]{1,0:T(8,128)(2,1)} %bitcast.9, bf16[8,64]{1,0:T(8,128)(2,1)} %gain_ref.1, bf16[64,1792]{1,0:T(8,128)(2,1)} %bitcast.10, ...), custom_call_target="tpu_custom_call" | custom-call | tf_op jit(solution)/shard_map/distill/pallas_call | solution.py:657
  86.2 1.4 %copy.17 = f32[28,256]{1,0:T(8,128)} copy(f32[28,256]{1,0:T(8,128)} %get-tuple-element.9) | data formatting | bytes 57344

commit v3 on v2

--- a/solution.py
+++ b/solution.py
@@ -60,6 +60,8 @@
         pvs=vmem((8, LEAD, KVW), BF16),
         pvr=vmem((8, LEAD, KVW), BF16),
         probs=vmem((2, 7 * LEAD, LEAD), BF16),
+        probs_t=vmem((2, LEAD, 7 * LEAD), BF16),
+        sb_t=vmem((KVW, 8 * LEAD), BF16),
         g1=vmem((8, LEAD, KVW), BF16),
         lost=vmem((8, 8, 128), F32),
         g2s=vmem((8, 32, KVW), BF16),
@@ -80,7 +82,7 @@
         psib_r=dma((8,)),
         **{
             name + end: dma((8,))
-            for name in ("py", "stu", "vwz", "vwy", "pv", "t5a", "t5b", "g1", "loss", "g2", "g3")
+            for name in ("stu", "vwz", "vwy", "pv", "t5a", "t5b", "g1", "loss", "g2", "g3")
             for end in ("_s", "_r")
         },
     )
@@ -297,20 +299,12 @@
     def half_block(owner, half):
         return m.proj.at[c, lax.rem(owner, 2), lax.div(owner, 2), pl.ds(32 * half, 32)]
 
-    def piece_at(place):
-        down, along = lax.div(place, 2), lax.rem(place, 2)
-        return pl.ds(pl.multiple_of(down * 16, 16), 16), pl.ds(pl.multiple_of(along * 896, 128), 896)
-
-    def piece(owner, place):
-        return m.proj.at[(c, lax.rem(owner, 2), lax.div(owner, 2)) + piece_at(place)]
-
     def pass_on(i, owner, half=None, src=None, **device):
         dst = block(owner) if half is None else half_block(owner, half)
         return remote(dst if src is None else src, dst, m.p_s.at[i], m.p_r.at[owner, half or 0], **device)
 
-    to_z = remote(proj_ref.at[piece_at(d)], piece(f, d), m.p_s.at[0], m.p_r.at[f, 0], fsdp=fz)
-    from_z = remote(proj_ref.at[piece_at(d)], piece(fz, d), m.p_s.at[0], m.p_r.at[fz, 0], fsdp=fz)
-    pieces = Exchange("dp", d, lambda peer: piece(fz, d), lambda slot: piece(fz, slot), m.py_s, m.py_r)
+    to_z = pass_on(0, f, src=proj_ref, fsdp=fz)
+    from_z = pass_on(0, fz, fsdp=fz)
     near_same = [pass_on(1, owner, fsdp=fz) for owner in (xm, xp)]
     near_other = [pass_on(1, owner, fsdp=fz) for owner in (xmz, xpz)]
     far_same = [pass_on(1, xf, half, fsdp=fz) for half in range(2)]
@@ -437,19 +431,22 @@
     flow.start(halves[1], due=[halves[1]])
     add_half(2)
     flow.start(*far, due=far)
+    flow.wait(from_z)
+    flow.start(pass_on(5, fz, fsdp=xp), pass_on(6, fz, fsdp=xm), due=near_other)
+    flow.wait(*near_same)
+    flow.start(pass_on(3, xm, 0, fsdp=xp), pass_on(4, xp, 1, fsdp=xm), due=far_same)
     partial(3)
     flow.start(halves[3], due=[halves[3]])
     add_half(1)
     flow.start(direct[0], due=direct[:1])
     proj_in.wait()
-    share(0)
-    flow.wait(from_z, sent_rows)
-    flow.start(pieces, due=[pieces])
     partial(0)
     flow.start(halves[0], due=[halves[0]])
     add_half(3)
     flow.start(direct[1], due=direct[1:])
+    flow.wait(sent_rows)
     flow.start(value_slices, due=[value_slices])
+    share(0, 1, 2, 4)
 
     resid_in.wait()
     row, col = iotas(512, 512)
@@ -464,12 +461,9 @@
     flow.start(resid_there, gain_there, due=[resid_here, gain_here])
     add_half(0)
 
-    flow.wait(*near_same)
-    flow.start(pass_on(3, xm, 0, fsdp=xp), pass_on(4, xp, 1, fsdp=xm), due=far_same)
-    share(1, 2)
-    flow.wait(pieces)
-    flow.start(pass_on(5, fz, fsdp=xp), pass_on(6, fz, fsdp=xm), due=near_other)
-    share(4)
+    flow.wait(*near_other)
+    flow.start(pass_on(7, xmz, 0, fsdp=xp), pass_on(8, xpz, 1, fsdp=xm), due=far_other)
+    share(5, 6)
     flow.wait(far[0])
     ring_sum(m.t1_added, 0, m.part[1, 0:64], m.t1_relay[0], 1024)
     flow.start(sums[0], due=sums[:1])
@@ -498,7 +492,9 @@
         scores = dot(jnp.concatenate(heads, axis=0), m.k[:, g * HEAD : (g + 1) * HEAD], ((1,), (1,)))
         scores = jnp.where(allow > 0.0, scores * HEAD ** (-0.5), -1e30)
         weights = jnp.exp(scores - jnp.max(scores, axis=1, keepdims=True))
-        m.probs[g] = (weights / jnp.sum(weights, axis=1, keepdims=True)).astype(BF16)
+        probs = weights / jnp.sum(weights, axis=1, keepdims=True)
+        m.probs[g] = probs.astype(BF16)
+        m.probs_t[g] = jnp.transpose(probs).astype(BF16)
 
     routes_in.wait()
     row, col = iotas(64, 32)
@@ -516,9 +512,8 @@
 
     flow.wait(*far_same)
     share(3)
-    flow.wait(*near_other)
-    flow.start(pass_on(7, xmz, 0, fsdp=xp), pass_on(8, xpz, 1, fsdp=xm), due=far_other)
-    share(5, 6)
+    flow.wait(*far_other)
+    share(7)
     flow.wait(*direct, *sums, resid_here, gain_here)
     flow.start(students, due=[students])
 
@@ -532,8 +527,6 @@
         power = power + jnp.sum(hidden * hidden, axis=1, keepdims=True)
         scaled.append((hidden * m.gainb[s, 0:1, :]).astype(BF16))
     m.pbuf0[:, :, CHUNKS[0] :] = split_sum(power).reshape(ZH, 32, 128)
-    flow.wait(*far_other)
-    share(7)
     flow.wait(*proj_here)
 
     def ahead(pbuf):
@@ -565,6 +558,7 @@
     value_part = dot(m.sb[...].reshape(8 * LEAD, KVW), rows_of_value)
     m.pvs[...] = value_part.reshape(8, LEAD, KVW).astype(BF16)
     m.pvr[f] = m.pvs[f]
+    m.sb_t[...] = jnp.transpose(m.sb[...].reshape(8 * LEAD, KVW).astype(F32)).astype(BF16)
 
     row_scale = None
     for i, name in enumerate(("t4a", "t4b")):
@@ -610,14 +604,14 @@
             lost = lost + masked * diff
             pieces_of[g].append((2.0 * masked / QW).astype(BF16))
     for g in range(2):
-        grad = dot(m.probs[g], jnp.concatenate(pieces_of[g], axis=0), ((0,), (0,)))
+        grad = dot(m.probs_t[g], jnp.concatenate(pieces_of[g], axis=0))
         m.g1[f, :, g * HEAD : (g + 1) * HEAD] = grad.astype(BF16)
     flow.start(grads1, due=[grads1])
     lost = lost.reshape(8, 8, 128).sum(axis=0)
     m.lost[f] = lost
     flow.start(losses, due=[losses])
     flow.wait(grads1)
-    grad = dot(m.sb[...].reshape(8 * LEAD, KVW), m.g1[...].reshape(8 * LEAD, KVW), ((0,), (0,)))
+    grad = dot(m.sb_t[...], m.g1[...].reshape(8 * LEAD, KVW))
     flow.wait(losses)
     tail = loss_row(jnp.sum(m.lost[...]))
     for j in range(N):

time: 89 us -> 86.4 us (0.971)
  Pallas kernels: 84.9 us -> 82.4 us
    pallas_call x1, Pallas kernels: 84.9 us -> 82.4 us  [local(): pl.pallas_call(functools.partial(kernel, float(16384 * QW), tuple(spec)),...]
where the time goes in v3:
time: 86.4 us; the launch traced here: 86.2 us
  Pallas kernels  82.4 us (95%)
  between operations  2.4 us (3%)
  local copies, waits for them, and re-layouts  1.38 us (2%)
    pallas_call x1, Pallas kernels, local(): pl.pallas_call(functools.partial(kernel, float(16384 * QW), tuple(spec)),...  82.4 us

profile of v3, /device:TPU:1, one launch (start us, length us, event | category | flops | bytes accessed | tf_op | source)
XLA Modules:
  0.0 86.2 jit_solution(17678750208320070518)
XLA Ops:
  0.6 82.4 %distill.1 = (f32[1,1]{1,0:T(1,128)}, f32[28,256]{1,0:T(8,128)}) custom-call(bf16[4,2,32,512]{3,2,1,0:T(8,128)(2,1)} %bitcast.8, s32[512,1024]{1,0:T(8,128)} %codes_ref.1, bf16[4,4096]{1,0:T(4,128)(2,1)} %scales_ref.1, bf16[512,256]{1,0:T(8,128)(2,1)} %bitcast.9, bf16[8,64]{1,0:T(8,128)(2,1)} %gain_ref.1, bf16[64,1792]{1,0:T(8,128)(2,1)} %bitcast.10, ...), custom_call_target="tpu_custom_call" | custom-call | tf_op jit(solution)/shard_map/distill/pallas_call | solution.py:651
  83.7 1.4 %copy.17 = f32[28,256]{1,0:T(8,128)} copy(f32[28,256]{1,0:T(8,128)} %get-tuple-element.9) | data formatting | bytes 57344

commit v4 on v3

--- a/solution.py
+++ b/solution.py
@@ -515,7 +515,6 @@
     flow.wait(*far_other)
     share(7)
     flow.wait(*direct, *sums, resid_here, gain_here)
-    flow.start(students, due=[students])
 
     lower = m.part[0, 0:64].astype(F32) + m.t1_summed[0].astype(F32) + m.t1_near[1].astype(F32)
     upper = m.part[0, 64:128].astype(F32) + m.t1_near[0].astype(F32) + m.t1_summed[1].astype(F32)
@@ -544,6 +543,7 @@
                 acc = acc + dot(scaled[s], jnp.concatenate(rows, axis=0))
             pbufs[i][:, :, lanes] = acc.astype(BF16).reshape(ZH, 32, 256)
         flow.start(*rings[i][0], *rings[i][1], due=rings[i][0] + rings[i][1])
+    flow.start(students, due=[students])
     for i, name in enumerate(("t4a", "t4b")):
         far4, direct4, sums4 = rings[i]
         relay, added = getattr(m, f"{name}_relay"), getattr(m, f"{name}_added")

time: 86.4 us -> 86.9 us (level)
  no operation moved by 1% of the time
where the time goes in v4:
time: 86.9 us; the launch traced here: 86.6 us
  Pallas kernels  82.9 us (95%)
  between operations  2.4 us (3%)
  local copies, waits for them, and re-layouts  1.38 us (2%)
    pallas_call x1, Pallas kernels, local(): pl.pallas_call(functools.partial(kernel, float(16384 * QW), tuple(spec)),...  82.9 us

profile of v4, /device:TPU:1, one launch (start us, length us, event | category | flops | bytes accessed | tf_op | source)
XLA Modules:
  0.0 86.6 jit_solution(6383678900988161612)
XLA Ops:
  0.6 82.9 %distill.1 = (f32[1,1]{1,0:T(1,128)}, f32[28,256]{1,0:T(8,128)}) custom-call(bf16[4,2,32,512]{3,2,1,0:T(8,128)(2,1)} %bitcast.8, s32[512,1024]{1,0:T(8,128)} %codes_ref.1, bf16[4,4096]{1,0:T(4,128)(2,1)} %scales_ref.1, bf16[512,256]{1,0:T(8,128)(2,1)} %bitcast.9, bf16[8,64]{1,0:T(8,128)(2,1)} %gain_ref.1, bf16[64,1792]{1,0:T(8,128)(2,1)} %bitcast.10, ...), custom_call_target="tpu_custom_call" | custom-call | tf_op jit(solution)/shard_map/distill/pallas_call | solution.py:651
  84.1 1.4 %copy.17 = f32[28,256]{1,0:T(8,128)} copy(f32[28,256]{1,0:T(8,128)} %get-tuple-element.9) | data formatting | bytes 57344
